TPU v7x, 32 devices: a whole 2x2x4 slice. The times are simulated.
32 devices in a mesh: parts: 2 (over y), tensor: 4 (over z), dp: 4 (over x, core).
Axes of the slice: x: 2, y: 2, z: 4, core: 2. Of those that a mesh axis runs over, the one named last changes fastest.
Arguments:
- layer_input_states: bfloat16 [4, 128, 5120], P(None, ('parts', 'dp'), 'tensor'), parts along dimension 1, may hold values from -80 to 80
- base_query_weight: bfloat16 [5120, 4096], P(None, 'tensor'), may hold values from -0.078125 to 0.078125
- key_value_weight: bfloat16 [5120, 1024], P('tensor'), may hold values from -0.078125 to 0.078125
- output_weight: bfloat16 [4096, 5120], P('tensor'), may hold values from -0.09375 to 0.09375
- stored_keys: bfloat16 [4, 128, 128, 128], P(None, ('parts', 'dp'), 'tensor'), parts along dimension 1, may hold values from -300 to 300
- stored_values: bfloat16 [4, 128, 128, 128], P(None, ('parts', 'dp'), 'tensor'), parts along dimension 1, may hold values from -6 to 6
- lengths: int32 [128], P(('parts', 'dp')), parts along dimension 0, may hold values from 4 to 124, as said below
- adapter_down: float32 [64, 10240], P(None, ('parts', 'tensor')), parts along dimension 1, may hold values from -0.078125 to 0.078125
- down_first_moment: float32 [64, 10240], P(None, ('parts', 'tensor')), parts along dimension 1, may hold values from -6 to 6
- down_second_moment: float32 [64, 10240], P(None, ('parts', 'tensor')), parts along dimension 1, may hold values from 0.5 to 20
- down_gradients: float32 [4, 64, 10240], P('dp', None, ('parts', 'tensor')), parts along dimension 2, may hold values from -6 to 6
- adapter_up: float32 [64, 8192], P(None, ('parts', 'tensor')), parts along dimension 1, may hold values from -0.375 to 0.375
- up_first_moment: float32 [64, 8192], P(None, ('parts', 'tensor')), parts along dimension 1, may hold values from -6 to 6
- up_second_moment: float32 [64, 8192], P(None, ('parts', 'tensor')), parts along dimension 1, may hold values from 0.5 to 20
- up_gradients: float32 [4, 64, 8192], P('dp', None, ('parts', 'tensor')), parts along dimension 2, may hold values from -6 to 6
Outputs:
- adapter_down_next: float32 [64, 10240], P(None, ('parts', 'tensor')), parts along dimension 1
- down_first_moment_next: float32 [64, 10240], P(None, ('parts', 'tensor')), parts along dimension 1
- down_second_moment_next: float32 [64, 10240], P(None, ('parts', 'tensor')), parts along dimension 1
- adapter_up_next: float32 [64, 8192], P(None, ('parts', 'tensor')), parts along dimension 1
- up_first_moment_next: float32 [64, 8192], P(None, ('parts', 'tensor')), parts along dimension 1
- up_second_moment_next: float32 [64, 8192], P(None, ('parts', 'tensor')), parts along dimension 1
- layer_out: bfloat16 [4, 128, 5120], P(None, ('parts', 'dp'), 'tensor'), parts along dimension 1
There are 2 independent parts, one for each index of `parts`. A program takes and returns all parts, laid end to end along the dimension named above; an argument that names none is the same for every part. Nothing has to cross between parts.
Inputs may be any that keep to these rules, and one draw needn't show every extreme that they name: `lengths`: the longest row reaches 124.
All inputs are finite; a program needn't handle non-finite values.
Results may differ from a plain program's by a relative error of at most 0.012.
The roundings to bfloat16 on the way count: a program that leaves them out, or rounds other values in their place, can miss the bound.
Values may be sent and summed in bfloat16 or wider, within the bound.
A program may use at most 128 MiB of HBM per device.

v0:
```python
import jax
import jax.numpy as jnp
from jax import lax
from jax.sharding import PartitionSpec as P

QUERY_HEAD_COUNT = 32
KEY_VALUE_HEADS = 4
HEAD_SIZE = 128


beta_one = 0.9
beta_two = 0.999
learn_rate = 0.01
adam_eps = 1e-08
bias_one = 1.0 - (0.9**50) ** 2
bias_two = 1.0 - (0.999**50) ** 2
adapter_scale = 2.0
norm_eps = 1e-06


def moment_optimizer_update(param, moment, second_moment, grad):
    moment_new = beta_one * moment + (1.0 - beta_one) * grad
    second_new = beta_two * second_moment + (1.0 - beta_two) * grad * grad
    step_size = moment_new / bias_one / (jnp.sqrt(second_new / bias_two) + adam_eps)
    return (param - learn_rate * step_size, moment_new, second_new)


def shards(
    layer_input_states,
    base_query_weight,
    key_value_weight,
    output_weight,
    stored_keys,
    stored_values,
    lengths,
    adapter_down,
    down_first_moment,
    down_second_moment,
    down_gradients,
    adapter_up,
    up_first_moment,
    up_second_moment,
    up_gradients,
):
    tensor_count = lax.axis_size("tensor")
    tensor_rank = lax.axis_index("tensor")
    summed_down_gradient, summed_up_gradient = lax.psum((down_gradients[0], up_gradients[0]), "dp")
    adapter_down_next, down_first_moment_next, down_second_moment_next = moment_optimizer_update(
        adapter_down, down_first_moment, down_second_moment, summed_down_gradient
    )
    adapter_up_next, up_first_moment_next, up_second_moment_next = moment_optimizer_update(
        adapter_up, up_first_moment, up_second_moment, summed_up_gradient
    )
    plain_query_rows = base_query_weight.astype(jnp.float32)
    factor_update = lax.dot_general(
        lax.all_gather(adapter_down_next, "tensor", axis=1, tiled=True),
        adapter_up_next,
        (((0,), (0,)), ((), ())),
        precision=lax.Precision.HIGHEST,
        preferred_element_type=jnp.float32,
    )
    merged_query_weight = (plain_query_rows + adapter_scale * factor_update).astype(jnp.bfloat16)
    heads_local = QUERY_HEAD_COUNT // tensor_count
    local_ctx = stored_keys.shape[2]
    slot_index = tensor_rank * local_ctx + jnp.arange(local_ctx, dtype=jnp.int32)
    score_scale = HEAD_SIZE ** (-0.5)
    key_cache = stored_keys
    value_cache = stored_values
    pieces = []
    for step_index in range(layer_input_states.shape[0]):
        hidden_block = layer_input_states[step_index : step_index + 1]
        decode_key_cache = key_cache
        decode_value_cache = value_cache
        optimizer_step_count = hidden_block.shape[0]
        decode_row_count = hidden_block.shape[1]
        gathered = lax.all_gather(hidden_block, "tensor", axis=2, tiled=True)
        widened = gathered.astype(jnp.float32)
        inverse = lax.rsqrt(jnp.mean(widened * widened, axis=-1, keepdims=True) + norm_eps)
        normed = (widened * inverse).astype(jnp.bfloat16)
        normed_local = (hidden_block.astype(jnp.float32) * inverse).astype(jnp.bfloat16)
        partial_kv = jnp.einsum(
            "srd,de->sre", normed_local, key_value_weight, preferred_element_type=jnp.float32
        )
        key_value_rows = lax.psum(partial_kv, "tensor").astype(jnp.bfloat16)
        key_value_rows = key_value_rows.reshape(
            optimizer_step_count, decode_row_count, 2, KEY_VALUE_HEADS, HEAD_SIZE
        )
        queries_local = jnp.einsum(
            "srd,de->sre", normed, merged_query_weight, preferred_element_type=jnp.float32
        ).astype(jnp.bfloat16)
        query_rows = lax.all_gather(queries_local, "tensor", axis=2, tiled=True)
        query_rows = query_rows.reshape(
            optimizer_step_count,
            decode_row_count,
            KEY_VALUE_HEADS,
            QUERY_HEAD_COUNT // KEY_VALUE_HEADS,
            HEAD_SIZE,
        )
        written = (slot_index[None, :] == lengths[:, None] + step_index + 0)[None, :, :, None]
        new_keys = jnp.transpose(key_value_rows[0, :, 0], (1, 0, 2))[:, :, None, :]
        new_values = jnp.transpose(key_value_rows[0, :, 1], (1, 0, 2))[:, :, None, :]
        decode_key_cache = jnp.where(written, new_keys, decode_key_cache)
        decode_value_cache = jnp.where(written, new_values, decode_value_cache)
        step_offsets = step_index + 1 + jnp.arange(optimizer_step_count, dtype=jnp.int32)
        visible = slot_index[None, None, :] < lengths[None, :, None] + step_offsets[:, None, None]
        visible = visible[:, None, None, :, :]
        scores = (
            jnp.einsum(
                "srhgd,hrcd->shgrc",
                query_rows,
                decode_key_cache,
                preferred_element_type=jnp.float32,
            )
            * score_scale
        )
        scores = jnp.where(visible, scores, -1e30)
        row_max = jnp.max(scores, axis=-1)
        weights = jnp.where(visible, jnp.exp(scores - row_max[..., None]), 0.0)
        totals = jnp.sum(weights, axis=-1)
        blended = jnp.einsum(
            "shgrc,hrcd->shgrd",
            weights.astype(jnp.bfloat16),
            decode_value_cache,
            preferred_element_type=jnp.float32,
        )
        blended = blended.reshape(
            optimizer_step_count, tensor_count, heads_local, decode_row_count, HEAD_SIZE
        )
        row_max = row_max.reshape(optimizer_step_count, tensor_count, heads_local, decode_row_count)
        totals = totals.reshape(optimizer_step_count, tensor_count, heads_local, decode_row_count)
        blended_in = lax.all_to_all(blended, "tensor", split_axis=1, concat_axis=1, tiled=True)
        peak_scores = lax.all_to_all(row_max, "tensor", split_axis=1, concat_axis=1, tiled=True)
        masses = lax.all_to_all(totals, "tensor", split_axis=1, concat_axis=1, tiled=True)
        overall = jnp.max(peak_scores, axis=1, keepdims=True)
        factor = jnp.exp(peak_scores - overall)
        denominator = jnp.sum(factor * masses, axis=1)
        combined = jnp.sum(factor[..., None] * blended_in, axis=1) / denominator[..., None]
        combined = jnp.transpose(combined, (0, 2, 1, 3))
        attended = combined.reshape(
            combined.shape[0], combined.shape[1], heads_local * HEAD_SIZE
        ).astype(jnp.bfloat16)
        projected = jnp.einsum(
            "sre,ed->srd", attended, output_weight, preferred_element_type=jnp.float32
        )
        reduced = lax.psum_scatter(projected, "tensor", scatter_dimension=2, tiled=True)
        step_out = reduced.astype(jnp.bfloat16)
        key_cache = decode_key_cache
        value_cache = decode_value_cache
        pieces.append(step_out)
    layer_out = jnp.concatenate(pieces, axis=0)
    return (
        adapter_down_next,
        down_first_moment_next,
        down_second_moment_next,
        adapter_up_next,
        up_first_moment_next,
        up_second_moment_next,
        layer_out,
    )


def solution(mesh):
    in_specs = (
        P(None, ("parts", "dp"), "tensor"),
        P(None, "tensor"),
        P("tensor", None),
        P("tensor", None),
        P(None, ("parts", "dp"), "tensor", None),
        P(None, ("parts", "dp"), "tensor", None),
        P(("parts", "dp")),
        P(None, ("parts", "tensor")),
        P(None, ("parts", "tensor")),
        P(None, ("parts", "tensor")),
        P("dp", None, ("parts", "tensor")),
        P(None, ("parts", "tensor")),
        P(None, ("parts", "tensor")),
        P(None, ("parts", "tensor")),
        P("dp", None, ("parts", "tensor")),
    )
    out_specs = (
        P(None, ("parts", "tensor")),
        P(None, ("parts", "tensor")),
        P(None, ("parts", "tensor")),
        P(None, ("parts", "tensor")),
        P(None, ("parts", "tensor")),
        P(None, ("parts", "tensor")),
        P(None, ("parts", "dp"), "tensor"),
    )
    return jax.shard_map(shards, mesh=mesh, in_specs=in_specs, out_specs=out_specs, check_vma=False)
```

profile of v0, /device:TPU:0, one launch (start us, length us, event | category | flops | bytes accessed | tf_op | source)
XLA Modules:
  0.0 389.9 jit_solution(13578001906567014412)
XLA Ops:
  8.8 15.1 %all_gather.34 = bf16[1,16,5120]{2,1,0:T(8,128)(2,1)S(1)} all-gather(bf16[1,16,1280]{2,1,0:T(8,128)(2,1)S(1)} %get-tuple-element.21), channel_id=1, replica_groups=mesh['parts'=2,'tensor'=4,'dp'=4] {'tensor'}, dimensions={2}, use_global_device_ids=true | all-gather | bytes 204800 | tf_op jit(solution)/shard_map/all_gather | solution.py:76
  25.4 13.7 %all_gather.32 = bf16[1,16,5120]{2,1,0:T(8,128)(2,1)S(1)} all-gather(bf16[1,16,1280]{2,1,0:T(8,128)(2,1)S(1)} %get-tuple-element.22), channel_id=1, replica_groups=mesh['parts'=2,'tensor'=4,'dp'=4] {'tensor'}, dimensions={2}, use_global_device_ids=true | all-gather | bytes 204800 | tf_op jit(solution)/shard_map/all_gather | solution.py:76
  40.5 13.5 %all_gather.30 = bf16[1,16,5120]{2,1,0:T(8,128)(2,1)S(1)} all-gather(bf16[1,16,1280]{2,1,0:T(8,128)(2,1)S(1)} %get-tuple-element.20), channel_id=1, replica_groups=mesh['parts'=2,'tensor'=4,'dp'=4] {'tensor'}, dimensions={2}, use_global_device_ids=true | all-gather | bytes 204800 | tf_op jit(solution)/shard_map/all_gather | solution.py:76
  55.5 14.0 %all_gather.27 = bf16[1,16,5120]{2,1,0:T(8,128)(2,1)S(1)} all-gather(bf16[1,16,1280]{2,1,0:T(8,128)(2,1)S(1)} %get-tuple-element.19), channel_id=1, replica_groups=mesh['parts'=2,'tensor'=4,'dp'=4] {'tensor'}, dimensions={2}, use_global_device_ids=true | all-gather | bytes 204800 | tf_op jit(solution)/shard_map/all_gather | solution.py:76
  73.3 29.1 %all-reduce.6 = (bf16[1,16,1024]{2,1,0:T(8,128)(2,1)}, bf16[1,16,1024]{2,1,0:T(8,128)(2,1)}, bf16[1,16,1024]{2,1,0:T(8,128)(2,1)}, bf16[1,16,1024]{2,1,0:T(8,128)(2,1)}) all-reduce(f32[1,16,1024]{2,1,0:T(8,128)S(1)} %convolution_bitcast_fusion.8, ...), channel_id=1, replica_groups=mesh['parts'=2,'tensor'=4,'dp'=4] {'tensor'}, use_global_device_ids=true, to_apply=%region_27.28 | all-reduce | flops 65536 | bytes 393216 | tf_op jit(solution)/shard_map/psum | solution.py:84
  114.0 19.9 %add_convert_fusion = bf16[5120,1024]{1,0:T(8,128)(2,1)S(1)} fusion(bf16[5120,1024]{1,0:T(8,128)(2,1)} %param.16, f32[64,5120]{1,0:T(8,128)} %all-gather.6.cloned.1.call-done, f32[64,1024]{1,0:T(8,128)S(1)} %get-tuple-element.13), kind=kOutput, calls=%fused_computation | convolution fusion | flops 4047503360 | bytes 22544384 | tf_op jit(solution)/shard_map/dot_general | solution.py:55
  140.1 13.3 %all-gather.3 = bf16[16,4096]{1,0:T(8,128)(2,1)S(1)} all-gather(bf16[16,1024]{1,0:T(8,128)(2,1)S(1)} %convolution_convert_fusion), channel_id=5, replica_groups=mesh['parts'=2,'tensor'=4,'dp'=4] {'tensor'}, dimensions={1}, use_global_device_ids=true | all-gather | bytes 163840 | tf_op jit(solution)/shard_map/all_gather | solution.py:91
  155.9 3.7 all-to-all-start.9
  159.7 14.2 %all-gather.2 = bf16[16,4096]{1,0:T(8,128)(2,1)S(1)} all-gather(bf16[16,1024]{1,0:T(8,128)(2,1)S(1)} %convolution_convert_fusion.1), channel_id=4, replica_groups=mesh['parts'=2,'tensor'=4,'dp'=4] {'tensor'}, dimensions={1}, use_global_device_ids=true | all-gather | bytes 163840 | tf_op jit(solution)/shard_map/all_gather | solution.py:91
  173.9 13.7 %all-gather.1 = bf16[16,4096]{1,0:T(8,128)(2,1)S(1)} all-gather(bf16[16,1024]{1,0:T(8,128)(2,1)S(1)} %convolution_convert_fusion.2), channel_id=3, replica_groups=mesh['parts'=2,'tensor'=4,'dp'=4] {'tensor'}, dimensions={1}, use_global_device_ids=true | all-gather | bytes 163840 | tf_op jit(solution)/shard_map/all_gather | solution.py:91
  187.6 13.4 %all-gather = bf16[16,4096]{1,0:T(8,128)(2,1)S(1)} all-gather(bf16[16,1024]{1,0:T(8,128)(2,1)S(1)} %convolution_convert_fusion.3), channel_id=2, replica_groups=mesh['parts'=2,'tensor'=4,'dp'=4] {'tensor'}, dimensions={1}, use_global_device_ids=true | all-gather | bytes 163840 | tf_op jit(solution)/shard_map/all_gather | solution.py:91
  213.5 4.6 %all-to-all-start.11 = ((f32[4,1,128]{2,1,0:T(1,128)}), f32[4,1,128]{2,1,0:T(1,128)S(1)}, u32[]{:S(2)}, u32[]{:S(2)}) async-start(f32[4,1,128]{2,1,0:T(1,128)} %reshape.641), calls=%async_computation.14 | async-start | bytes 4096 | tf_op jit(solution)/shard_map/all_to_all | solution.py:133
  223.5 3.2 all-to-all-start.6
  232.1 3.3 all-to-all-start.8
  241.3 5.1 %all-to-all-start.3 = ((f32[4,1,128]{2,1,0:T(1,128)}), f32[4,1,128]{2,1,0:T(1,128)S(1)}, u32[]{:S(2)}, u32[]{:S(2)}) async-start(f32[4,1,128]{2,1,0:T(1,128)} %reshape.647), calls=%async_computation.4 | async-start | bytes 4096 | tf_op jit(solution)/shard_map/all_to_all | solution.py:132
  247.0 4.7 %all-to-all-done.3 = f32[4,1,128]{2,1,0:T(1,128)S(1)} async-done(((f32[4,1,128]{2,1,0:T(1,128)}), f32[4,1,128]{2,1,0:T(1,128)S(1)}, u32[]{:S(2)}, u32[]{:S(2)}) %all-to-all-start.3) | async-done | bytes 2080 | tf_op jit(solution)/shard_map/all_to_all | solution.py:132
  255.6 4.8 %all-to-all-done.5 = f32[4,1,128]{2,1,0:T(1,128)S(1)} async-done(((f32[4,1,128]{2,1,0:T(1,128)}), f32[4,1,128]{2,1,0:T(1,128)S(1)}, u32[]{:S(2)}, u32[]{:S(2)}) %all-to-all-start.5) | async-done | bytes 2080 | tf_op jit(solution)/shard_map/all_to_all | solution.py:133
  264.3 4.8 %all-to-all-done = f32[4,1,128]{2,1,0:T(1,128)S(1)} async-done(((f32[4,1,128]{2,1,0:T(1,128)}), f32[4,1,128]{2,1,0:T(1,128)S(1)}, u32[]{:S(2)}, u32[]{:S(2)}) %all-to-all-start) | async-done | bytes 2080 | tf_op jit(solution)/shard_map/all_to_all | solution.py:132
  269.1 3.2 all-to-all-start.2
  273.1 4.7 %all-to-all-done.2 = f32[4,1,128]{2,1,0:T(1,128)S(1)} async-done(((f32[4,1,128]{2,1,0:T(1,128)}), f32[4,1,128]{2,1,0:T(1,128)S(1)}, u32[]{:S(2)}, u32[]{:S(2)}) %all-to-all-start.2) | async-done | bytes 2080 | tf_op jit(solution)/shard_map/all_to_all | solution.py:133
  277.7 3.4 all-to-all-start.10
  283.8 4.1 %all-to-all-done.10 = f32[1,4,8,16,128]{4,2,3,0,1:T(8,128)S(1)} async-done(((f32[1,4,8,16,128]{4,2,3,0,1:T(8,128)}), f32[1,4,8,16,128]{4,2,3,0,1:T(8,128)S(1)}, u32[]{:S(2)}, u32[]{:S(2)}) %all-to-all-start.10) | async-done | bytes 262176 | tf_op jit(solution)/shard_map/all_to_all | solution.py:131
  287.9 3.4 all-to-all-start.7
  291.6 6.2 %convolution_bitcast_fusion = f32[1,16,5120]{2,1,0:T(8,128)} fusion(bf16[1024,5120]{1,0:T(8,128)(2,1)} %param.18, bf16[2,8,8,128]{3,2,1,0:T(8,128)(2,1)S(1)} %bitcast.258), kind=kOutput, calls=%fused_computation.1 | convolution fusion | flops 167772160 | bytes 10846208 | tf_op jit(solution)/shard_map/sre,ed->srd/dot_general | solution.py:142
  298.1 4.8 %all-to-all-start.4 = ((f32[1,4,8,16,128]{4,2,3,0,1:T(8,128)}), f32[1,4,8,16,128]{4,2,3,0,1:T(8,128)S(1)}, u32[]{:S(2)}, u32[]{:S(2)}) async-start(f32[1,4,8,16,128]{4,2,3,0,1:T(8,128)} %convolution_bitcast_fusion.6), calls=%async_computation.5 | async-start | bytes 524288 | tf_op jit(solution)/shard_map/all_to_all | solution.py:131
  303.1 6.3 %convolution_bitcast_fusion.1 = f32[1,16,5120]{2,1,0:T(8,128)} fusion(bf16[1024,5120]{1,0:T(8,128)(2,1)} %param.18, bf16[2,8,8,128]{3,2,1,0:T(8,128)(2,1)S(1)} %bitcast.259), kind=kOutput, calls=%fused_computation.2 | convolution fusion | flops 167772160 | bytes 10846208 | tf_op jit(solution)/shard_map/sre,ed->srd/dot_general | solution.py:142
  311.5 3.4 all-to-all-start.1
  315.2 6.2 %convolution_bitcast_fusion.2 = f32[1,16,5120]{2,1,0:T(8,128)} fusion(bf16[1024,5120]{1,0:T(8,128)(2,1)} %param.18, bf16[2,8,8,128]{3,2,1,0:T(8,128)(2,1)S(1)} %bitcast.260), kind=kOutput, calls=%fused_computation.3 | convolution fusion | flops 167772160 | bytes 10846208 | tf_op jit(solution)/shard_map/sre,ed->srd/dot_general | solution.py:142
  322.0 6.2 %convolution_bitcast_fusion.3 = f32[1,16,5120]{2,1,0:T(8,128)} fusion(bf16[1024,5120]{1,0:T(8,128)(2,1)} %param.18, bf16[2,8,8,128]{3,2,1,0:T(8,128)(2,1)S(1)} %bitcast.261), kind=kOutput, calls=%fused_computation.4 | convolution fusion | flops 167772160 | bytes 10846208 | tf_op jit(solution)/shard_map/sre,ed->srd/dot_general | solution.py:142
  329.1 11.5 %reduce-scatter.9.cloned.1.call-done = f32[1,16,1280]{2,1,0:T(8,128)} async-done(((f32[1,16,5120]{2,1,0:T(8,128)}), f32[1,16,1280]{2,1,0:T(8,128)}) %reduce-scatter.9.cloned.1.call-update) | async-done | bytes 81936 | tf_op jit(solution)/shard_map/reduce_scatter | solution.py:145
  341.6 19.5 %reduce-scatter.7.cloned.1.call-done = f32[1,16,1280]{2,1,0:T(8,128)} async-done(((f32[1,16,5120]{2,1,0:T(8,128)}), f32[1,16,1280]{2,1,0:T(8,128)}) %reduce-scatter.7.cloned.1.call-update) | async-done | bytes 81936 | tf_op jit(solution)/shard_map/reduce_scatter | solution.py:145
  361.9 19.5 %reduce-scatter.5.cloned.1.call-done = f32[1,16,1280]{2,1,0:T(8,128)} async-done(((f32[1,16,5120]{2,1,0:T(8,128)}), f32[1,16,1280]{2,1,0:T(8,128)}) %reduce-scatter.5.cloned.1.call-update) | async-done | bytes 81936 | tf_op jit(solution)/shard_map/reduce_scatter | solution.py:145
  (186 shorter events, 78.5 us)
Async XLA Ops:
  7.2 17.0 %copy-start = (bf16[1280,1024]{1,0:T(8,128)(2,1)S(1)}, bf16[1280,1024]{1,0:T(8,128)(2,1)}, u32[]{:S(2)}) copy-start(bf16[1280,1024]{1,0:T(8,128)(2,1)} %param.17) | copy-start | bytes 7864324
  7.2 62.5 %all-reduce.5.cloned.1.call-start = ((), (), s32[]{:S(2)}) async-start(), calls=%async_computation.21 | async-start | bytes 1179648 | tf_op jit(solution)/shard_map/psum | solution.py:47
  7.9 106.1 %all-gather.6.cloned.1.call-start = ((), (), s32[]{:S(2)}) async-start(), calls=%async_computation.16 | async-start | bytes 1638400 | tf_op jit(solution)/shard_map/all_gather | solution.py:56
  24.1 31.3 %copy-start.10 = (f32[16]{0:T(128)}, f32[16]{0:T(128)S(1)}, u32[]{:S(2)}) copy-start(f32[16]{0:T(128)S(1)} %add_rsqrt_fusion) | copy-start | bytes 196
  39.3 16.2 %copy-start.12 = (f32[16]{0:T(128)}, f32[16]{0:T(128)S(1)}, u32[]{:S(2)}) copy-start(f32[16]{0:T(128)S(1)} %add_rsqrt_fusion.1) | copy-start | bytes 196
  69.6 37.8 %copy-start.16 = (f32[16]{0:T(128)}, f32[16]{0:T(128)S(1)}, u32[]{:S(2)}) copy-start(f32[16]{0:T(128)S(1)} %add_rsqrt_fusion.3) | copy-start | bytes 196
  114.0 19.9 %copy-start.1 = (f32[64,1024]{1,0:T(8,128)}, f32[64,1024]{1,0:T(8,128)S(1)}, u32[]{:S(2)}) copy-start(f32[64,1024]{1,0:T(8,128)S(1)} %get-tuple-element.13) | copy-start | bytes 786436
  114.0 19.9 %copy-start.11 = (f32[16]{0:T(128)S(1)}, f32[16]{0:T(128)}, u32[]{:S(2)}) copy-start(f32[16]{0:T(128)} %copy-done.10) | copy-start | bytes 196
  138.5 15.0 %copy-start.6 = (bf16[4,16,128]{2,1,0:T(8,128)(2,1)S(1)}, bf16[4,16,128]{2,1,0:T(8,128)(2,1)}, u32[]{:S(2)}) copy-start(bf16[4,16,128]{2,1,0:T(8,128)(2,1)} %copy.78) | copy-start | bytes 49156
  138.5 15.0 %copy-start.7 = (bf16[4,16,128]{2,1,0:T(8,128)(2,1)S(1)}, bf16[4,16,128]{2,1,0:T(8,128)(2,1)}, u32[]{:S(2)}) copy-start(bf16[4,16,128]{2,1,0:T(8,128)(2,1)} %copy.86) | copy-start | bytes 49156
  138.5 15.0 %copy-start.8 = (bf16[4,16,128]{2,1,0:T(8,128)(2,1)S(1)}, bf16[4,16,128]{2,1,0:T(8,128)(2,1)}, u32[]{:S(2)}) copy-start(bf16[4,16,128]{2,1,0:T(8,128)(2,1)} %copy.94) | copy-start | bytes 49156
  138.5 15.0 %copy-start.9 = (pred[16,32]{1,0:T(8,128)(4,1)S(1)}, pred[16,32]{1,0:T(8,128)(4,1)}, u32[]{:S(2)}) copy-start(pred[16,32]{1,0:T(8,128)(4,1)} %get-tuple-element.50) | copy-start | bytes 1540
  138.6 64.2 %copy-start.2 = (bf16[4,16,128]{2,1,0:T(8,128)(2,1)S(1)}, bf16[4,16,128]{2,1,0:T(8,128)(2,1)}, u32[]{:S(2)}) copy-start(bf16[4,16,128]{2,1,0:T(8,128)(2,1)} %copy.82) | copy-start | bytes 49156
  138.6 64.2 %copy-start.3 = (bf16[4,16,128]{2,1,0:T(8,128)(2,1)S(1)}, bf16[4,16,128]{2,1,0:T(8,128)(2,1)}, u32[]{:S(2)}) copy-start(bf16[4,16,128]{2,1,0:T(8,128)(2,1)} %copy.98) | copy-start | bytes 49156
  138.6 64.2 %copy-start.4 = (bf16[4,16,128]{2,1,0:T(8,128)(2,1)S(1)}, bf16[4,16,128]{2,1,0:T(8,128)(2,1)}, u32[]{:S(2)}) copy-start(bf16[4,16,128]{2,1,0:T(8,128)(2,1)} %copy.90) | copy-start | bytes 49156
  155.9 57.6 %all-to-all-start.9 = ((f32[4,1,128]{2,1,0:T(1,128)}), f32[4,1,128]{2,1,0:T(1,128)}, u32[]{:S(2)}, u32[]{:S(2)}) async-start(f32[4,1,128]{2,1,0:T(1,128)} %reshape.639), calls=%async_computation.12 | async-start | bytes 4096 | tf_op jit(solution)/shard_map/all_to_all | solution.py:132
  159.7 49.4 %copy-start.23 = (bf16[4,16,32,128]{3,2,1,0:T(8,128)(2,1)S(1)}, bf16[4,16,32,128]{3,2,1,0:T(8,128)(2,1)}, u32[]{:S(2)}) copy-start(bf16[4,16,32,128]{3,2,1,0:T(8,128)(2,1)} %param.19) | copy-start | bytes 1572868
  213.5 9.9 %all-to-all-start.11 = ((f32[4,1,128]{2,1,0:T(1,128)}), f32[4,1,128]{2,1,0:T(1,128)S(1)}, u32[]{:S(2)}, u32[]{:S(2)}) async-start(f32[4,1,128]{2,1,0:T(1,128)} %reshape.641), calls=%async_computation.14 | async-start | bytes 4096 | tf_op jit(solution)/shard_map/all_to_all | solution.py:133
  223.5 8.6 %all-to-all-start.6 = ((f32[4,1,128]{2,1,0:T(1,128)}), f32[4,1,128]{2,1,0:T(1,128)S(1)}, u32[]{:S(2)}, u32[]{:S(2)}) async-start(f32[4,1,128]{2,1,0:T(1,128)} %reshape.643), calls=%async_computation.8 | async-start | bytes 4096 | tf_op jit(solution)/shard_map/all_to_all | solution.py:132
  232.1 9.2 %all-to-all-start.8 = ((f32[4,1,128]{2,1,0:T(1,128)}), f32[4,1,128]{2,1,0:T(1,128)S(1)}, u32[]{:S(2)}, u32[]{:S(2)}) async-start(f32[4,1,128]{2,1,0:T(1,128)} %reshape.645), calls=%async_computation.10 | async-start | bytes 4096 | tf_op jit(solution)/shard_map/all_to_all | solution.py:133
  241.3 10.5 %all-to-all-start.3 = ((f32[4,1,128]{2,1,0:T(1,128)}), f32[4,1,128]{2,1,0:T(1,128)S(1)}, u32[]{:S(2)}, u32[]{:S(2)}) async-start(f32[4,1,128]{2,1,0:T(1,128)} %reshape.647), calls=%async_computation.4 | async-start | bytes 4096 | tf_op jit(solution)/shard_map/all_to_all | solution.py:132
  251.8 8.7 %all-to-all-start.5 = ((f32[4,1,128]{2,1,0:T(1,128)}), f32[4,1,128]{2,1,0:T(1,128)S(1)}, u32[]{:S(2)}, u32[]{:S(2)}) async-start(f32[4,1,128]{2,1,0:T(1,128)} %reshape.649), calls=%async_computation.6 | async-start | bytes 4096 | tf_op jit(solution)/shard_map/all_to_all | solution.py:133
  260.5 8.7 %all-to-all-start = ((f32[4,1,128]{2,1,0:T(1,128)}), f32[4,1,128]{2,1,0:T(1,128)S(1)}, u32[]{:S(2)}, u32[]{:S(2)}) async-start(f32[4,1,128]{2,1,0:T(1,128)} %reshape.651), calls=%async_computation | async-start | bytes 4096 | tf_op jit(solution)/shard_map/all_to_all | solution.py:132
  269.1 8.6 %all-to-all-start.2 = ((f32[4,1,128]{2,1,0:T(1,128)}), f32[4,1,128]{2,1,0:T(1,128)S(1)}, u32[]{:S(2)}, u32[]{:S(2)}) async-start(f32[4,1,128]{2,1,0:T(1,128)} %reshape.653), calls=%async_computation.2 | async-start | bytes 4096 | tf_op jit(solution)/shard_map/all_to_all | solution.py:133
  277.7 10.2 %all-to-all-start.10 = ((f32[1,4,8,16,128]{4,2,3,0,1:T(8,128)}), f32[1,4,8,16,128]{4,2,3,0,1:T(8,128)S(1)}, u32[]{:S(2)}, u32[]{:S(2)}) async-start(f32[1,4,8,16,128]{4,2,3,0,1:T(8,128)} %convolution_bitcast_fusion.4), calls=%async_computation.13 | async-start | bytes 524288 | tf_op jit(solution)/shard_map/all_to_all | solution.py:131
  287.9 10.2 %all-to-all-start.7 = ((f32[1,4,8,16,128]{4,2,3,0,1:T(8,128)}), f32[1,4,8,16,128]{4,2,3,0,1:T(8,128)S(1)}, u32[]{:S(2)}, u32[]{:S(2)}) async-start(f32[1,4,8,16,128]{4,2,3,0,1:T(8,128)} %convolution_bitcast_fusion.5), calls=%async_computation.9 | async-start | bytes 524288 | tf_op jit(solution)/shard_map/all_to_all | solution.py:131
  291.3 36.9 %reduce-scatter.11.cloned.1.call-start = ((), (), s32[]{:S(2)}) async-start(), calls=%async_computation.20 | async-start | bytes 409600 | tf_op jit(solution)/shard_map/reduce_scatter | solution.py:145
  298.1 13.4 %all-to-all-start.4 = ((f32[1,4,8,16,128]{4,2,3,0,1:T(8,128)}), f32[1,4,8,16,128]{4,2,3,0,1:T(8,128)S(1)}, u32[]{:S(2)}, u32[]{:S(2)}) async-start(f32[1,4,8,16,128]{4,2,3,0,1:T(8,128)} %convolution_bitcast_fusion.6), calls=%async_computation.5 | async-start | bytes 524288 | tf_op jit(solution)/shard_map/all_to_all | solution.py:131
  302.9 37.8 %reduce-scatter.9.cloned.1.call-start = ((), (), s32[]{:S(2)}) async-start(), calls=%async_computation.19 | async-start | bytes 409600 | tf_op jit(solution)/shard_map/reduce_scatter | solution.py:145
  311.5 10.2 %all-to-all-start.1 = ((f32[1,4,8,16,128]{4,2,3,0,1:T(8,128)}), f32[1,4,8,16,128]{4,2,3,0,1:T(8,128)S(1)}, u32[]{:S(2)}, u32[]{:S(2)}) async-start(f32[1,4,8,16,128]{4,2,3,0,1:T(8,128)} %convolution_bitcast_fusion.7), calls=%async_computation.1 | async-start | bytes 524288 | tf_op jit(solution)/shard_map/all_to_all | solution.py:131
  315.0 46.1 %reduce-scatter.7.cloned.1.call-start = ((), (), s32[]{:S(2)}) async-start(), calls=%async_computation.18 | async-start | bytes 409600 | tf_op jit(solution)/shard_map/reduce_scatter | solution.py:145
  321.5 60.0 %reduce-scatter.5.cloned.1.call-start = ((), (), s32[]{:S(2)}) async-start(), calls=%async_computation.17 | async-start | bytes 409600 | tf_op jit(solution)/shard_map/reduce_scatter | solution.py:145
  (10 other events, 95.9 us)
Sparse Core Ops, SparseCore 0:
  10.5 36.2 all-reduce.4
  72.1 37.1 all-gather.5
  297.9 22.0 reduce-scatter.10
  322.1 18.4 reduce-scatter.8
  342.8 18.1 reduce-scatter.6
  363.2 18.2 reduce-scatter.4
where the time goes:
time: 392 us; the launch traced here: 390 us
  blocking collectives  140 us (36%)
  waiting for transfers between devices  81.4 us (21%)
  matrix products  70.9 us (18%)
  starting transfers between devices  44.7 us (11%)
  other arithmetic  20.5 us (5%)
  local copies, waits for them, and re-layouts  17.6 us (4%)
  between operations  14.7 us (4%)
    all_gather x4, blocking collectives, shards(): gathered = lax.all_gather(hidden_block, 'tensor', axis=2, tiled=True)  56.3 us
    all_gather x4, blocking collectives, shards(): query_rows = lax.all_gather(queries_local, 'tensor', axis=2, tiled=True)  54.6 us
    reduce_scatter x4, waiting for transfers between devices, shards(): lax.psum_scatter(projected, 'tensor', scatter_dimension=2, tiled=True)  50.6 us
    psum x1, blocking collectives, shards(): key_value_rows = lax.psum(partial_kv, 'tensor').astype(jnp.bfloat16)  29.1 us
    dot_general x4, matrix products, shards(): jnp.einsum('sre,ed->srd', attended, output_weight, preferred_element_type...  24.8 us
    dot_general x1, matrix products, shards(): lax.dot_general(lax.all_gather(adapter_down_next, 'tensor', axis=1, tiled...  19.9 us
    all_to_all x4, starting transfers between devices, shards(): lax.all_to_all(row_max, 'tensor', split_axis=1, concat_axis=1, tiled=True)  15.2 us
    all_to_all x4, starting transfers between devices, shards(): lax.all_to_all(blended, 'tensor', split_axis=1, concat_axis=1, tiled=True)  15 us
  transfers between devices with their start and end apart: 18, of which 13 were waited for; matrix products, arithmetic and copies ran while one was open for 20% of the time, Pallas kernels for 0%

commit v1 on v0

--- a/solution.py
+++ b/solution.py
@@ -1,6 +1,10 @@
+import functools
+
 import jax
 import jax.numpy as jnp
 from jax import lax
+from jax.experimental import pallas as pl
+from jax.experimental.pallas import tpu as pltpu
 from jax.sharding import PartitionSpec as P
 
 QUERY_HEAD_COUNT = 32
@@ -25,7 +29,7 @@
     return (param - learn_rate * step_size, moment_new, second_new)
 
 
-def shards(
+def general_shards(
     layer_input_states,
     base_query_weight,
     key_value_weight,
@@ -159,7 +163,458 @@
     )
 
 
+MESH = pl.DeviceIdType.MESH
+F32 = jnp.float32
+BF16 = jnp.bfloat16
+
+
+def split_high_low(value):
+    high = value.astype(BF16)
+    return high, (value - high.astype(F32)).astype(BF16)
+
+
+def fused_kernel(
+    shards_z,
+    x_in,
+    base_in,
+    kvw_in,
+    ow_in,
+    keys_in,
+    values_in,
+    lengths_ref,
+    pd_in,
+    md_in,
+    vd_in,
+    gd_in,
+    pu_in,
+    mu_in,
+    vu_in,
+    gu_in,
+    pd_out,
+    md_out,
+    vd_out,
+    pu_out,
+    mu_out,
+    vu_out,
+    layer_out,
+    xg,
+    normed,
+    base_v,
+    kvw_v,
+    ow_v,
+    keys_v,
+    values_v,
+    pd,
+    md,
+    vd,
+    pu,
+    mu,
+    vu,
+    gd,
+    gu,
+    g1d,
+    g1u,
+    g2d,
+    g2u,
+    r2d,
+    r2u,
+    gsd,
+    gsu,
+    factors,
+    up_cat,
+    kv_send,
+    kv_recv,
+    q_acc,
+    q_rows,
+    blend_rows,
+    att,
+    out_send,
+    out_recv,
+    out_final,
+    load_sem,
+    store_sem,
+    z_send,
+    z_recv,
+    pair_send,
+    pair_recv,
+):
+    t = lax.axis_index("tensor")
+    replica = lax.axis_index("dp")
+    half = lax.rem(replica, 2)
+    other = 1 - half
+    mate = replica + 1 - 2 * half
+    across = lax.rem(replica + 2, 4)
+    rank = pd.shape[0]
+    hr = rank // 2
+    width = xg.shape[2]
+    steps_rows = xg.shape[1]
+    mine = pl.ds(pl.multiple_of(half * hr, hr), hr)
+    theirs = pl.ds(pl.multiple_of(other * hr, hr), hr)
+    peers = [lax.rem(t + d, shards_z) for d in range(1, shards_z)]
+    sources = [lax.rem(t + shards_z - d, shards_z) for d in range(1, shards_z)]
+    order = range(shards_z - 1)
+
+    def load(index, src, dst):
+        copy = pltpu.make_async_copy(src, dst, load_sem.at[index])
+        copy.start()
+        return copy
+
+    def to_z(kind, d, src, dst):
+        copy = pltpu.make_async_remote_copy(
+            src_ref=src,
+            dst_ref=dst,
+            send_sem=z_send.at[kind, d],
+            recv_sem=z_recv.at[kind, d],
+            device_id={"tensor": peers[d]},
+            device_id_type=MESH,
+        )
+        copy.start()
+        return copy
+
+    def to_dp(index, target, src, dst):
+        copy = pltpu.make_async_remote_copy(
+            src_ref=src,
+            dst_ref=dst,
+            send_sem=pair_send.at[index],
+            recv_sem=pair_recv.at[index],
+            device_id={"dp": target},
+            device_id_type=MESH,
+        )
+        copy.start()
+        return copy
+
+    barrier = pltpu.get_barrier_semaphore()
+    for p in peers:
+        pl.semaphore_signal(barrier, inc=1, device_id={"tensor": p}, device_id_type=MESH)
+    for p in (mate, across):
+        pl.semaphore_signal(barrier, inc=1, device_id={"dp": p}, device_id_type=MESH)
+    load_gd = load(0, gd_in, gd)
+    load_gu = load(1, gu_in, gu)
+    adam_loads = [
+        load(2 + i, a, b)
+        for i, (a, b) in enumerate(
+            ((pd_in, pd), (md_in, md), (vd_in, vd), (pu_in, pu), (mu_in, mu), (vu_in, vu))
+        )
+    ]
+    load_x = load(8, x_in, xg.at[t])
+    load_kvw = load(9, kvw_in, kvw_v)
+    load_base = load(10, base_in, base_v)
+    load_keys = load(11, keys_in.at[t], keys_v.at[t])
+    load_values = load(12, values_in.at[t], values_v.at[t])
+    load_ow = load(13, ow_in, ow_v)
+    pl.semaphore_wait(barrier, shards_z + 1)
+
+    g1 = [
+        to_dp(0, mate, gd_in.at[theirs], g1d),
+        to_dp(1, mate, gu_in.at[theirs], g1u),
+    ]
+    sent_x = [to_z(0, d, x_in, xg.at[t]) for d in order]
+
+    load_gd.wait()
+    load_gu.wait()
+    for copy in g1:
+        copy.wait_recv()
+    g2d[...] = gd[mine, :] + g1d[...]
+    g2u[...] = gu[mine, :] + g1u[...]
+    g2 = [to_dp(2, across, g2d, r2d), to_dp(3, across, g2u, r2u)]
+    for copy in adam_loads:
+        copy.wait()
+    for copy in g2:
+        copy.wait_recv()
+    gsd[mine, :] = g2d[...] + r2d[...]
+    gsu[mine, :] = g2u[...] + r2u[...]
+    gs = [
+        to_dp(4, mate, gsd.at[mine], gsd.at[mine]),
+        to_dp(5, mate, gsu.at[mine], gsu.at[mine]),
+    ]
+
+    def step_down(rows, which):
+        new = moment_optimizer_update(pd[rows, :], md[rows, :], vd[rows, :], gsd[rows, :])
+        pd[rows, :], md[rows, :], vd[rows, :] = new
+        high, low = split_high_low(new[0])
+        factors[t, which, 0:hr, :] = high
+        factors[t, which, hr : 2 * hr, :] = low
+
+    step_down(mine, half)
+    sent_factors = [to_z(1, d, factors.at[t, half], factors.at[t, half]) for d in order]
+    sent_keys = [to_z(3, d, keys_in.at[peers[d]], keys_v.at[t]) for d in order]
+    sent_values = [to_z(4, d, values_in.at[peers[d]], values_v.at[t]) for d in order]
+
+    for copy in gs:
+        copy.wait_recv()
+    step_down(theirs, other)
+    new_up = moment_optimizer_update(pu[...], mu[...], vu[...], gsu[...])
+    pu[...], mu[...], vu[...] = new_up
+    stores = []
+    for i, (a, b) in enumerate(
+        ((pd, pd_out), (md, md_out), (vd, vd_out), (pu, pu_out), (mu, mu_out), (vu, vu_out))
+    ):
+        copy = pltpu.make_async_copy(a, b, store_sem.at[i])
+        copy.start()
+        stores.append(copy)
+    up_parts = split_high_low(adapter_scale * new_up[0])
+    for i in range(2):
+        for j in range(2):
+            piece = up_parts[i][j * hr : (j + 1) * hr, :]
+            at = (i * 2 + j) * 2 * hr
+            up_cat[at : at + hr, :] = piece
+            up_cat[at + hr : at + 2 * hr, :] = piece
+
+    load_x.wait()
+    for copy in sent_x:
+        copy.wait_recv()
+    squares = jnp.zeros((steps_rows, 1), F32)
+    for b in range(shards_z):
+        wide = xg[b].astype(F32)
+        squares = squares + jnp.sum(wide * wide, axis=-1, keepdims=True)
+    inverse = lax.rsqrt(squares / (width * shards_z) + norm_eps)
+    for b in range(shards_z):
+        normed[b] = (xg[b].astype(F32) * inverse).astype(BF16)
+    load_kvw.wait()
+    local_rows = normed[t]
+    kv_half = KEY_VALUE_HEADS * HEAD_SIZE
+    for p in range(shards_z):
+        for kind in range(2):
+            at = kind * kv_half + p * HEAD_SIZE
+            kv_send[p, :, kind * HEAD_SIZE : (kind + 1) * HEAD_SIZE] = jnp.dot(
+                local_rows, kvw_v[:, at : at + HEAD_SIZE], preferred_element_type=F32
+            )
+    sent_kv = [to_z(2, d, kv_send.at[peers[d]], kv_recv.at[t]) for d in order]
+
+    load_base.wait()
+    q_acc[...] = jnp.zeros_like(q_acc)
+    tile = 256
+
+    def query_block(b):
+        def body(j, carry):
+            columns = pl.ds(pl.multiple_of(j * tile, tile), tile)
+            left = factors[b, :, :, columns].reshape(2 * rank, tile)
+            update = lax.dot_general(
+                jnp.concatenate([left, left], axis=0),
+                up_cat[...],
+                (((0,), (0,)), ((), ())),
+                preferred_element_type=F32,
+            )
+            rows = pl.ds(pl.multiple_of(b * width + j * tile, tile), tile)
+            merged = (base_v[rows, :].astype(F32) + update).astype(BF16)
+            q_acc[...] += jnp.dot(normed[b, :, columns], merged, preferred_element_type=F32)
+            return carry
+
+        lax.fori_loop(0, width // tile, body, 0)
+
+    query_block(t)
+    passed = []
+    for d in order:
+        sent_factors[d].wait_recv()
+        slot = factors.at[sources[d], half]
+        passed.append(to_dp(6 + d, mate, slot, slot))
+    for d in order:
+        passed[d].wait_recv()
+        query_block(sources[d])
+
+    rows_each = q_rows.shape[0]
+    steps = steps_rows // rows_each
+    group = q_acc.shape[1] // HEAD_SIZE
+    rounded = q_acc[...].astype(BF16).astype(F32)
+    for s in range(steps):
+        for g in range(group):
+            q_rows[:, s * group + g, :] = rounded[
+                s * rows_each : (s + 1) * rows_each, g * HEAD_SIZE : (g + 1) * HEAD_SIZE
+            ]
+    for copy in sent_kv:
+        copy.wait_recv()
+    new_kv = kv_send[t]
+    for d in order:
+        new_kv = new_kv + kv_recv[sources[d]]
+    new_kv = new_kv.astype(BF16)
+    new_keys = new_kv[:, :HEAD_SIZE]
+    new_values = new_kv[:, HEAD_SIZE:]
+    load_keys.wait()
+    load_values.wait()
+    for copy in sent_keys + sent_values:
+        copy.wait_recv()
+    queries = q_rows[...].astype(BF16)
+    keys = jnp.concatenate([keys_v[b] for b in range(shards_z)], axis=1)
+    values = jnp.concatenate([values_v[b] for b in range(shards_z)], axis=1)
+    scale = HEAD_SIZE ** (-0.5)
+    pairs = steps * group
+    old = (
+        lax.dot_general(
+            queries, keys, (((2,), (2,)), ((0,), (0,))), preferred_element_type=F32
+        )
+        * scale
+    )
+    fresh = (
+        lax.dot_general(
+            queries.reshape(rows_each * pairs, HEAD_SIZE),
+            new_keys,
+            (((1,), (1,)), ((), ())),
+            preferred_element_type=F32,
+        )
+        * scale
+    ).reshape(rows_each, pairs, steps_rows)
+    place = lax.broadcasted_iota(jnp.int32, old.shape, 2)
+    seen_old = place < lengths_ref[...]
+    column = lax.broadcasted_iota(jnp.int32, fresh.shape, 2)
+    row = lax.broadcasted_iota(jnp.int32, fresh.shape, 0)
+    step = lax.broadcasted_iota(jnp.int32, fresh.shape, 1) // group
+    seen_new = (column % rows_each == row) & (column // rows_each <= step)
+    old = jnp.where(seen_old, old, -1e30)
+    fresh = jnp.where(seen_new, fresh, -1e30)
+    peak = jnp.maximum(
+        jnp.max(old, axis=-1, keepdims=True), jnp.max(fresh, axis=-1, keepdims=True)
+    )
+    old = jnp.where(seen_old, jnp.exp(old - peak), 0.0)
+    fresh = jnp.where(seen_new, jnp.exp(fresh - peak), 0.0)
+    total = jnp.sum(old, axis=-1, keepdims=True) + jnp.sum(fresh, axis=-1, keepdims=True)
+    blended = lax.dot_general(
+        old.astype(BF16), values, (((2,), (1,)), ((0,), (0,))), preferred_element_type=F32
+    )
+    blended = blended + jnp.dot(
+        fresh.reshape(rows_each * pairs, steps_rows).astype(BF16),
+        new_values,
+        preferred_element_type=F32,
+    ).reshape(rows_each, pairs, HEAD_SIZE)
+    blend_rows[...] = blended / total
+    for s in range(steps):
+        for g in range(group):
+            att[
+                s * rows_each : (s + 1) * rows_each, g * HEAD_SIZE : (g + 1) * HEAD_SIZE
+            ] = blend_rows[:, s * group + g, :].astype(BF16)
+
+    load_ow.wait()
+
+    def project(p):
+        columns = pl.ds(pl.multiple_of(p * width, 128), width)
+        return jnp.dot(att[...], ow_v[:, columns], preferred_element_type=F32)
+
+    sent_out = []
+    for d in order:
+        out_send[d] = project(peers[d]).astype(BF16)
+        sent_out.append(to_z(5, d, out_send.at[d], out_recv.at[d]))
+    result = project(t)
+    for d in order:
+        sent_out[d].wait_recv()
+        result = result + out_recv[d].astype(F32)
+    out_final[...] = result.astype(BF16)
+    last = pltpu.make_async_copy(out_final, layer_out, store_sem.at[6])
+    last.start()
+    for copy in (
+        g1 + g2 + gs + passed + sent_x + sent_factors + sent_keys + sent_values + sent_kv + sent_out
+    ):
+        copy.wait_send()
+    for copy in stores:
+        copy.wait()
+    last.wait()
+
+
+def fused_shards(
+    layer_input_states,
+    base_query_weight,
+    key_value_weight,
+    output_weight,
+    stored_keys,
+    stored_values,
+    lengths,
+    adapter_down,
+    down_first_moment,
+    down_second_moment,
+    down_gradients,
+    adapter_up,
+    up_first_moment,
+    up_second_moment,
+    up_gradients,
+):
+    z = lax.axis_size("tensor")
+    steps, rows, width = layer_input_states.shape
+    rank = adapter_down.shape[0]
+    columns = base_query_weight.shape[1]
+    group = columns // HEAD_SIZE
+    flat = steps * rows
+    context = stored_keys.shape[2]
+    place = jax.ShapeDtypeStruct
+    down = adapter_down.shape
+    up = adapter_up.shape
+    down_half = (rank // 2, down[1])
+    up_half = (rank // 2, up[1])
+    seen = jnp.broadcast_to(lengths[:, None, None], (rows, steps * group, z * context))
+    whole = pl.BlockSpec(memory_space=pl.ANY)
+    in_specs = [whole] * 6 + [pl.BlockSpec(memory_space=pltpu.VMEM)] + [whole] * 8
+    vm = pltpu.VMEM
+    dma = pltpu.SemaphoreType.DMA
+    results = pl.pallas_call(
+        functools.partial(fused_kernel, z),
+        out_shape=[place(down, F32)] * 3 + [place(up, F32)] * 3 + [place((flat, width), BF16)],
+        in_specs=in_specs,
+        out_specs=[whole] * 7,
+        scratch_shapes=[
+            vm((z, flat, width), BF16),
+            vm((z, flat, width), BF16),
+            vm(base_query_weight.shape, BF16),
+            vm(key_value_weight.shape, BF16),
+            vm(output_weight.shape, BF16),
+            vm((z, rows, context, HEAD_SIZE), BF16),
+            vm((z, rows, context, HEAD_SIZE), BF16),
+            vm(down, F32),
+            vm(down, F32),
+            vm(down, F32),
+            vm(up, F32),
+            vm(up, F32),
+            vm(up, F32),
+            vm(down, F32),
+            vm(up, F32),
+            vm(down_half, F32),
+            vm(up_half, F32),
+            vm(down_half, F32),
+            vm(up_half, F32),
+            vm(down_half, F32),
+            vm(up_half, F32),
+            vm(down, F32),
+            vm(up, F32),
+            vm((z, 2, rank, width), BF16),
+            vm((4 * rank, columns), BF16),
+            vm((z, flat, 2 * HEAD_SIZE), F32),
+            vm((z, flat, 2 * HEAD_SIZE), F32),
+            vm((flat, columns), F32),
+            vm((rows, steps * group, HEAD_SIZE), F32),
+            vm((rows, steps * group, HEAD_SIZE), F32),
+            vm((flat, columns), BF16),
+            vm((z - 1, flat, width), BF16),
+            vm((z - 1, flat, width), BF16),
+            vm((flat, width), BF16),
+            dma((14,)),
+            dma((7,)),
+            dma((6, z - 1)),
+            dma((6, z - 1)),
+            dma((6 + z - 1,)),
+            dma((6 + z - 1,)),
+        ],
+        compiler_params=pltpu.CompilerParams(
+            collective_id=0, has_side_effects=True, vmem_limit_bytes=56 * 1024 * 1024
+        ),
+    )(
+        layer_input_states.reshape(flat, width),
+        base_query_weight,
+        key_value_weight,
+        output_weight,
+        stored_keys,
+        stored_values,
+        seen,
+        adapter_down,
+        down_first_moment,
+        down_second_moment,
+        down_gradients[0],
+        adapter_up,
+        up_first_moment,
+        up_second_moment,
+        up_gradients[0],
+    )
+    return (*results[:6], results[6].reshape(steps, rows, width))
+
+
 def solution(mesh):
+    local_heads = KEY_VALUE_HEADS == mesh.shape["tensor"] and mesh.shape["dp"] == 4
+    shards = fused_shards if local_heads else general_shards
     in_specs = (
         P(None, ("parts", "dp"), "tensor"),
         P(None, "tensor"),

time: 392 us -> 93.3 us (0.24)
  blocking collectives: 140 us -> 0 us
  waiting for transfers between devices: 81.4 us -> 0 us
  Pallas kernels: 0 us -> 79.1 us
  matrix products: 70.9 us -> 0 us
  starting transfers between devices: 44.7 us -> 0 us
  other arithmetic: 20.5 us -> 0 us
  between operations: 14.7 us -> 0.64 us
  local copies, waits for them, and re-layouts: 17.6 us -> 13.2 us
    all_gather x8 -> x0, blocking collectives: 111 us -> none  [the longest x4 56.3 us: shards(): gathered = lax.all_gather(hidden_block, 'tensor', axis=2, tiled=True)]
    pallas_call x0 -> x1, Pallas kernels: none -> 79.1 us  [fused_shards(): pl.pallas_call(functools.partial(fused_kernel, z), out_shape=[place(down,...]
    dot_general x21 -> x0, matrix products: 70.9 us -> none  [the longest x4 24.8 us: shards(): jnp.einsum('sre,ed->srd', attended, output_weight, preferred_element_type...]
    reduce_scatter x4 -> x0, waiting for transfers between devices: 50.6 us -> none  [shards(): lax.psum_scatter(projected, 'tensor', scatter_dimension=2, tiled=True)]
    all_to_all x12 -> x0, starting transfers between devices: 44.5 us -> none  [the longest x4 15.2 us: shards(): lax.all_to_all(row_max, 'tensor', split_axis=1, concat_axis=1, tiled=True)]
    all_to_all x12 -> x0, waiting for transfers between devices: 30.1 us -> none  [the longest x4 12 us: shards(): lax.all_to_all(totals, 'tensor', split_axis=1, concat_axis=1, tiled=True)]
    psum x1 -> x0, blocking collectives: 29.1 us -> none  [shards(): key_value_rows = lax.psum(partial_kv, 'tensor').astype(jnp.bfloat16)]
    unnamed x68 -> x7, local copies, waits for them, and re-layouts: 6.21 us -> 11.8 us
  transfers between devices with their start and end apart: 18 -> 0, of which waited for: 13 -> 0; matrix products, arithmetic and copies ran while one was open for 20% -> 0% of each run, Pallas kernels for 0% -> 0%
where the time goes in v1:
time: 93.3 us; the launch traced here: 92.9 us
  Pallas kernels  79.1 us (85%)
  local copies, waits for them, and re-layouts  13.2 us (14%)
    pallas_call x1, Pallas kernels, fused_shards(): pl.pallas_call(functools.partial(fused_kernel, z), out_shape=[place(down,...  79.1 us
    unnamed x7, local copies, waits for them, and re-layouts  11.8 us

profile of v1, /device:TPU:0, one launch (start us, length us, event | category | flops | bytes accessed | tf_op | source)
XLA Modules:
  0.0 92.9 jit_solution(10423759718602092805)
XLA Ops:
  0.6 1.4 %broadcast_in_dim.2.lengths_ref = s32[16,32,128]{2,1,0:T(8,128)} broadcast(s32[16]{0:T(128)} %param.21), dimensions={0} | broadcast | bytes 262208 | tf_op jit(solution)/shard_map/broadcast_in_dim | solution.py:540
  2.1 79.1 %shard_map.198 = (f32[64,1280]{1,0:T(8,128)}, f32[64,1280]{1,0:T(8,128)}, f32[64,1280]{1,0:T(8,128)}, f32[64,1024]{1,0:T(8,128)}, f32[64,1024]{1,0:T(8,128)}, /*...) custom-call(bf16[64,1280]{1,0:T(8,128)(2,1)} %bitcast.6, bf16[5120,1024]{1,0:T(8,128)(2,1)} %base_in.1, ...), custom_call_target="tpu_custom_call" | custom-call | tf_op jit(solution)/shard_map/pallas_call | solution.py:545
  81.2 1.7 %copy.29 = f32[64,1280]{1,0:T(8,128)} copy(f32[64,1280]{1,0:T(8,128)} %get-tuple-element.28) | data formatting | bytes 655360
  82.9 1.7 %copy.30 = f32[64,1280]{1,0:T(8,128)} copy(f32[64,1280]{1,0:T(8,128)} %get-tuple-element.29) | data formatting | bytes 655360
  84.6 1.7 %copy.31 = f32[64,1280]{1,0:T(8,128)} copy(f32[64,1280]{1,0:T(8,128)} %get-tuple-element.30) | data formatting | bytes 655360
  86.3 1.7 %copy.32 = f32[64,1024]{1,0:T(8,128)} copy(f32[64,1024]{1,0:T(8,128)} %get-tuple-element.31) | data formatting | bytes 524288
  88.0 1.7 %copy.33 = f32[64,1024]{1,0:T(8,128)} copy(f32[64,1024]{1,0:T(8,128)} %get-tuple-element.32) | data formatting | bytes 524288
  89.7 1.7 %copy.34 = f32[64,1024]{1,0:T(8,128)} copy(f32[64,1024]{1,0:T(8,128)} %get-tuple-element.33) | data formatting | bytes 524288
  91.3 1.6 %copy.35 = bf16[4,16,1280]{2,1,0:T(8,128)(2,1)} copy(bf16[4,16,1280]{2,1,0:T(8,128)(2,1)} %bitcast.7) | data formatting | bytes 327680

commit v2 on v1

--- a/solution.py
+++ b/solution.py
@@ -230,6 +230,7 @@
     att,
     out_send,
     out_recv,
+    out_wide,
     out_final,
     load_sem,
     store_sem,
@@ -237,6 +238,8 @@
     z_recv,
     pair_send,
     pair_recv,
+    hop_send,
+    hop_recv,
 ):
     t = lax.axis_index("tensor")
     replica = lax.axis_index("dp")
@@ -246,8 +249,16 @@
     across = lax.rem(replica + 2, 4)
     rank = pd.shape[0]
     hr = rank // 2
+    qr = rank // 4
+    side = replica // 2
+    quarter = half * 2 + side
+    beside = half * 2 + 1 - side
     width = xg.shape[2]
     steps_rows = xg.shape[1]
+
+    def quarter_rows(q):
+        return pl.ds(pl.multiple_of(q * qr, qr), qr)
+
     mine = pl.ds(pl.multiple_of(half * hr, hr), hr)
     theirs = pl.ds(pl.multiple_of(other * hr, hr), hr)
     peers = [lax.rem(t + d, shards_z) for d in range(1, shards_z)]
@@ -282,6 +293,46 @@
         )
         copy.start()
         return copy
+
+    def hop_copy(way, k, block, first):
+        return pltpu.make_async_remote_copy(
+            src_ref=x_in if first else xg.at[block],
+            dst_ref=xg.at[block],
+            send_sem=hop_send.at[way, k - 1],
+            recv_sem=hop_recv.at[way, k - 1],
+            device_id={"tensor": peers[0] if way == 0 else sources[0]},
+            device_id_type=MESH,
+        )
+
+    def hop_sends(way, k):
+        if way == 0:
+            return (t < shards_z - 1) & (t >= k - 1), sources[k - 2] if k > 1 else t
+        return (t > 0) & (t + k <= shards_z), peers[k - 2] if k > 1 else t
+
+    def hop_start(k):
+        for way in range(2):
+            sends, block = hop_sends(way, k)
+
+            @pl.when(sends)
+            def _(way=way, block=block):
+                hop_copy(way, k, block, k == 1).start()
+
+    def hop_finish(k):
+        for way in range(2):
+            sends, block = hop_sends(way, k)
+
+            @pl.when(sends)
+            def _(way=way, block=block):
+                hop_copy(way, k, block, k == 1).wait_send()
+
+    def hop_arrive(k):
+        for way in range(2):
+            gets = t >= k if way == 0 else t + k < shards_z
+
+            @pl.when(gets)
+            def _(way=way):
+                block = sources[k - 1] if way == 0 else peers[k - 1]
+                hop_copy(way, k, block, False).wait_recv()
 
     barrier = pltpu.get_barrier_semaphore()
     for p in peers:
@@ -308,7 +359,7 @@
         to_dp(0, mate, gd_in.at[theirs], g1d),
         to_dp(1, mate, gu_in.at[theirs], g1u),
     ]
-    sent_x = [to_z(0, d, x_in, xg.at[t]) for d in order]
+    hop_start(1)
 
     load_gd.wait()
     load_gu.wait()
@@ -316,33 +367,64 @@
         copy.wait_recv()
     g2d[...] = gd[mine, :] + g1d[...]
     g2u[...] = gu[mine, :] + g1u[...]
-    g2 = [to_dp(2, across, g2d, r2d), to_dp(3, across, g2u, r2u)]
+    kept = quarter_rows(side)
+    given = quarter_rows(1 - side)
+    g2 = [to_dp(2, across, g2d.at[given], r2d), to_dp(3, across, g2u.at[given], r2u)]
+    hop_arrive(1)
+    hop_start(2)
     for copy in adam_loads:
         copy.wait()
     for copy in g2:
         copy.wait_recv()
-    gsd[mine, :] = g2d[...] + r2d[...]
-    gsu[mine, :] = g2u[...] + r2u[...]
+    own = quarter_rows(quarter)
+    next_to = quarter_rows(beside)
+    gsd[own, :] = g2d[kept, :] + r2d[...]
+    gsu[own, :] = g2u[kept, :] + r2u[...]
     gs = [
-        to_dp(4, mate, gsd.at[mine], gsd.at[mine]),
-        to_dp(5, mate, gsu.at[mine], gsu.at[mine]),
+        to_dp(4, across, gsd.at[own], gsd.at[own]),
+        to_dp(5, across, gsu.at[own], gsu.at[own]),
     ]
-
-    def step_down(rows, which):
+    gm = [
+        to_dp(6, mate, gsd.at[own], gsd.at[own]),
+        to_dp(7, mate, gsu.at[own], gsu.at[own]),
+    ]
+
+    def step_down(q):
+        rows = quarter_rows(q)
         new = moment_optimizer_update(pd[rows, :], md[rows, :], vd[rows, :], gsd[rows, :])
         pd[rows, :], md[rows, :], vd[rows, :] = new
         high, low = split_high_low(new[0])
-        factors[t, which, 0:hr, :] = high
-        factors[t, which, hr : 2 * hr, :] = low
-
-    step_down(mine, half)
-    sent_factors = [to_z(1, d, factors.at[t, half], factors.at[t, half]) for d in order]
-    sent_keys = [to_z(3, d, keys_in.at[peers[d]], keys_v.at[t]) for d in order]
-    sent_values = [to_z(4, d, values_in.at[peers[d]], values_v.at[t]) for d in order]
-
+        factors[t, q, 0:qr, :] = high
+        factors[t, q, qr : 2 * qr, :] = low
+
+    step_down(quarter)
+    sent_factors = [to_z(0, d, factors.at[t, quarter], factors.at[t, quarter]) for d in order]
+    hop_arrive(2)
+    hop_start(3)
+    parts_of_rows = 2
+    rows_each = q_rows.shape[0]
+    rows_part = rows_each // parts_of_rows
+
+    def send_caches(part):
+        cut = pl.ds(part * rows_part, rows_part)
+        return [
+            to_z(2 + 2 * part + i, d, source.at[peers[d], cut], held.at[t, cut])
+            for d in order
+            for i, (source, held) in enumerate(((keys_in, keys_v), (values_in, values_v)))
+        ]
+
+    sent_caches = [send_caches(0)]
     for copy in gs:
         copy.wait_recv()
-    step_down(theirs, other)
+    gm += [
+        to_dp(8, mate, gsd.at[next_to], gsd.at[next_to]),
+        to_dp(9, mate, gsu.at[next_to], gsu.at[next_to]),
+    ]
+    step_down(beside)
+    for copy in gm:
+        copy.wait_recv()
+    step_down(other * 2)
+    step_down(other * 2 + 1)
     new_up = moment_optimizer_update(pu[...], mu[...], vu[...], gsu[...])
     pu[...], mu[...], vu[...] = new_up
     stores = []
@@ -354,15 +436,14 @@
         stores.append(copy)
     up_parts = split_high_low(adapter_scale * new_up[0])
     for i in range(2):
-        for j in range(2):
-            piece = up_parts[i][j * hr : (j + 1) * hr, :]
-            at = (i * 2 + j) * 2 * hr
-            up_cat[at : at + hr, :] = piece
-            up_cat[at + hr : at + 2 * hr, :] = piece
+        for j in range(4):
+            piece = up_parts[i][j * qr : (j + 1) * qr, :]
+            at = (i * 4 + j) * 2 * qr
+            up_cat[at : at + qr, :] = piece
+            up_cat[at + qr : at + 2 * qr, :] = piece
 
     load_x.wait()
-    for copy in sent_x:
-        copy.wait_recv()
+    hop_arrive(3)
     squares = jnp.zeros((steps_rows, 1), F32)
     for b in range(shards_z):
         wide = xg[b].astype(F32)
@@ -379,7 +460,8 @@
             kv_send[p, :, kind * HEAD_SIZE : (kind + 1) * HEAD_SIZE] = jnp.dot(
                 local_rows, kvw_v[:, at : at + HEAD_SIZE], preferred_element_type=F32
             )
-    sent_kv = [to_z(2, d, kv_send.at[peers[d]], kv_recv.at[t]) for d in order]
+    sent_kv = [to_z(1, d, kv_send.at[peers[d]], kv_recv.at[t]) for d in order]
+    sent_caches.append(send_caches(1))
 
     load_base.wait()
     q_acc[...] = jnp.zeros_like(q_acc)
@@ -404,15 +486,21 @@
 
     query_block(t)
     passed = []
+    crossed = []
     for d in order:
         sent_factors[d].wait_recv()
-        slot = factors.at[sources[d], half]
-        passed.append(to_dp(6 + d, mate, slot, slot))
+        slot = factors.at[sources[d], quarter]
+        crossed.append(to_dp(10 + 3 * d, across, slot, slot))
+        passed.append(to_dp(11 + 3 * d, mate, slot, slot))
+    for d in order:
+        crossed[d].wait_recv()
+        slot = factors.at[sources[d], beside]
+        passed.append(to_dp(12 + 3 * d, mate, slot, slot))
     for d in order:
         passed[d].wait_recv()
+        passed[shards_z - 1 + d].wait_recv()
         query_block(sources[d])
 
-    rows_each = q_rows.shape[0]
     steps = steps_rows // rows_each
     group = q_acc.shape[1] // HEAD_SIZE
     rounded = q_acc[...].astype(BF16).astype(F32)
@@ -431,81 +519,113 @@
     new_values = new_kv[:, HEAD_SIZE:]
     load_keys.wait()
     load_values.wait()
-    for copy in sent_keys + sent_values:
-        copy.wait_recv()
-    queries = q_rows[...].astype(BF16)
-    keys = jnp.concatenate([keys_v[b] for b in range(shards_z)], axis=1)
-    values = jnp.concatenate([values_v[b] for b in range(shards_z)], axis=1)
+    load_ow.wait()
     scale = HEAD_SIZE ** (-0.5)
     pairs = steps * group
-    old = (
-        lax.dot_general(
-            queries, keys, (((2,), (2,)), ((0,), (0,))), preferred_element_type=F32
-        )
-        * scale
-    )
-    fresh = (
-        lax.dot_general(
-            queries.reshape(rows_each * pairs, HEAD_SIZE),
-            new_keys,
-            (((1,), (1,)), ((), ())),
-            preferred_element_type=F32,
-        )
-        * scale
-    ).reshape(rows_each, pairs, steps_rows)
-    place = lax.broadcasted_iota(jnp.int32, old.shape, 2)
-    seen_old = place < lengths_ref[...]
-    column = lax.broadcasted_iota(jnp.int32, fresh.shape, 2)
-    row = lax.broadcasted_iota(jnp.int32, fresh.shape, 0)
-    step = lax.broadcasted_iota(jnp.int32, fresh.shape, 1) // group
-    seen_new = (column % rows_each == row) & (column // rows_each <= step)
-    old = jnp.where(seen_old, old, -1e30)
-    fresh = jnp.where(seen_new, fresh, -1e30)
-    peak = jnp.maximum(
-        jnp.max(old, axis=-1, keepdims=True), jnp.max(fresh, axis=-1, keepdims=True)
-    )
-    old = jnp.where(seen_old, jnp.exp(old - peak), 0.0)
-    fresh = jnp.where(seen_new, jnp.exp(fresh - peak), 0.0)
-    total = jnp.sum(old, axis=-1, keepdims=True) + jnp.sum(fresh, axis=-1, keepdims=True)
-    blended = lax.dot_general(
-        old.astype(BF16), values, (((2,), (1,)), ((0,), (0,))), preferred_element_type=F32
-    )
-    blended = blended + jnp.dot(
-        fresh.reshape(rows_each * pairs, steps_rows).astype(BF16),
-        new_values,
-        preferred_element_type=F32,
-    ).reshape(rows_each, pairs, HEAD_SIZE)
-    blend_rows[...] = blended / total
-    for s in range(steps):
-        for g in range(group):
-            att[
-                s * rows_each : (s + 1) * rows_each, g * HEAD_SIZE : (g + 1) * HEAD_SIZE
-            ] = blend_rows[:, s * group + g, :].astype(BF16)
-
-    load_ow.wait()
+    flat_part = rows_part * pairs
+    steps_part = steps * rows_part
+    sent_out = []
+    results = []
 
     def project(p):
         columns = pl.ds(pl.multiple_of(p * width, 128), width)
-        return jnp.dot(att[...], ow_v[:, columns], preferred_element_type=F32)
-
-    sent_out = []
-    for d in order:
-        out_send[d] = project(peers[d]).astype(BF16)
-        sent_out.append(to_z(5, d, out_send.at[d], out_recv.at[d]))
-    result = project(t)
-    for d in order:
-        sent_out[d].wait_recv()
-        result = result + out_recv[d].astype(F32)
-    out_final[...] = result.astype(BF16)
+        return jnp.dot(att[...].astype(BF16), ow_v[:, columns], preferred_element_type=F32)
+
+    for part in range(parts_of_rows):
+        for copy in sent_caches[part]:
+            copy.wait_recv()
+        cut = slice(part * rows_part, (part + 1) * rows_part)
+        queries = q_rows[cut].astype(BF16)
+        keys = jnp.concatenate([keys_v[b, cut] for b in range(shards_z)], axis=1)
+        values = jnp.concatenate([values_v[b, cut] for b in range(shards_z)], axis=1)
+        old = (
+            lax.dot_general(
+                queries, keys, (((2,), (2,)), ((0,), (0,))), preferred_element_type=F32
+            )
+            * scale
+        )
+        fresh = (
+            lax.dot_general(
+                queries.reshape(flat_part, HEAD_SIZE),
+                new_keys,
+                (((1,), (1,)), ((), ())),
+                preferred_element_type=F32,
+            )
+            * scale
+        ).reshape(rows_part, pairs, steps_rows)
+        place = lax.broadcasted_iota(jnp.int32, old.shape, 2)
+        filled = [
+            jnp.full((1, 1, old.shape[2]), lengths_ref[part * rows_part + r], jnp.int32)
+            for r in range(rows_part)
+        ]
+        seen_old = place < jnp.concatenate(filled, axis=0)
+        column = lax.broadcasted_iota(jnp.int32, fresh.shape, 2)
+        row = lax.broadcasted_iota(jnp.int32, fresh.shape, 0) + part * rows_part
+        step = lax.broadcasted_iota(jnp.int32, fresh.shape, 1) // group
+        seen_new = (column % rows_each == row) & (column // rows_each <= step)
+        old = jnp.where(seen_old, old, -1e30)
+        fresh = jnp.where(seen_new, fresh, -1e30)
+        peak = jnp.maximum(
+            jnp.max(old, axis=-1, keepdims=True), jnp.max(fresh, axis=-1, keepdims=True)
+        )
+        old = jnp.where(seen_old, jnp.exp(old - peak), 0.0)
+        fresh = jnp.where(seen_new, jnp.exp(fresh - peak), 0.0)
+        total = jnp.sum(old, axis=-1, keepdims=True) + jnp.sum(fresh, axis=-1, keepdims=True)
+        blended = lax.dot_general(
+            old.astype(BF16), values, (((2,), (1,)), ((0,), (0,))), preferred_element_type=F32
+        )
+        blended = blended + jnp.dot(
+            fresh.reshape(flat_part, steps_rows).astype(BF16),
+            new_values,
+            preferred_element_type=F32,
+        ).reshape(rows_part, pairs, HEAD_SIZE)
+        blend_rows[...] = blended / total
+        for s in range(steps):
+            for g in range(group):
+                att[
+                    s * rows_part : (s + 1) * rows_part, g * HEAD_SIZE : (g + 1) * HEAD_SIZE
+                ] = blend_rows[:, s * group + g, :]
+        for d in order:
+            out_send[part, d] = project(peers[d]).astype(BF16)
+            sent_out.append(
+                to_z(6 + part, d, out_send.at[part, d], out_recv.at[part, d])
+            )
+        results.append(project(t))
+    for part in range(parts_of_rows):
+        result = results[part]
+        for d in order:
+            sent_out[part * (shards_z - 1) + d].wait_recv()
+            result = result + out_recv[part, d].astype(F32)
+        for s in range(steps):
+            at = s * rows_each + part * rows_part
+            out_wide[at : at + rows_part, :] = result[s * rows_part : (s + 1) * rows_part, :]
+    out_final[...] = out_wide[...].astype(BF16)
     last = pltpu.make_async_copy(out_final, layer_out, store_sem.at[6])
     last.start()
-    for copy in (
-        g1 + g2 + gs + passed + sent_x + sent_factors + sent_keys + sent_values + sent_kv + sent_out
-    ):
+    for k in range(1, shards_z):
+        hop_finish(k)
+    for copy in g1 + g2 + gs + gm + passed + crossed + sent_factors + sent_kv + sent_out:
         copy.wait_send()
+    for copies in sent_caches:
+        for copy in copies:
+            copy.wait_send()
     for copy in stores:
         copy.wait()
     last.wait()
+
+
+def write_kernel(count, *refs):
+    sources, targets, held = (refs[i * count : (i + 1) * count] for i in range(3))
+    sem = refs[-1]
+    reads = [pltpu.make_async_copy(sources[i], held[i], sem.at[0, i]) for i in range(count)]
+    writes = [pltpu.make_async_copy(held[i], targets[i], sem.at[1, i]) for i in range(count)]
+    for copy in reads:
+        copy.start()
+    for read, write in zip(reads, writes):
+        read.wait()
+        write.start()
+    for copy in writes:
+        copy.wait()
 
 
 def fused_shards(
@@ -537,9 +657,8 @@
     up = adapter_up.shape
     down_half = (rank // 2, down[1])
     up_half = (rank // 2, up[1])
-    seen = jnp.broadcast_to(lengths[:, None, None], (rows, steps * group, z * context))
     whole = pl.BlockSpec(memory_space=pl.ANY)
-    in_specs = [whole] * 6 + [pl.BlockSpec(memory_space=pltpu.VMEM)] + [whole] * 8
+    in_specs = [whole] * 6 + [pl.BlockSpec(memory_space=pltpu.SMEM)] + [whole] * 8
     vm = pltpu.VMEM
     dma = pltpu.SemaphoreType.DMA
     results = pl.pallas_call(
@@ -567,27 +686,30 @@
             vm(up_half, F32),
             vm(down_half, F32),
             vm(up_half, F32),
-            vm(down_half, F32),
-            vm(up_half, F32),
+            vm((rank // 4, down[1]), F32),
+            vm((rank // 4, up[1]), F32),
             vm(down, F32),
             vm(up, F32),
-            vm((z, 2, rank, width), BF16),
+            vm((z, 4, rank // 2, width), BF16),
             vm((4 * rank, columns), BF16),
             vm((z, flat, 2 * HEAD_SIZE), F32),
             vm((z, flat, 2 * HEAD_SIZE), F32),
             vm((flat, columns), F32),
             vm((rows, steps * group, HEAD_SIZE), F32),
-            vm((rows, steps * group, HEAD_SIZE), F32),
-            vm((flat, columns), BF16),
-            vm((z - 1, flat, width), BF16),
-            vm((z - 1, flat, width), BF16),
+            vm((rows // 2, steps * group, HEAD_SIZE), F32),
+            vm((flat // 2, columns), F32),
+            vm((2, z - 1, flat // 2, width), BF16),
+            vm((2, z - 1, flat // 2, width), BF16),
+            vm((flat, width), F32),
             vm((flat, width), BF16),
             dma((14,)),
             dma((7,)),
-            dma((6, z - 1)),
-            dma((6, z - 1)),
-            dma((6 + z - 1,)),
-            dma((6 + z - 1,)),
+            dma((8, z - 1)),
+            dma((8, z - 1)),
+            dma((10 + 3 * (z - 1),)),
+            dma((10 + 3 * (z - 1),)),
+            dma((2, z - 1)),
+            dma((2, z - 1)),
         ],
         compiler_params=pltpu.CompilerParams(
             collective_id=0, has_side_effects=True, vmem_limit_bytes=56 * 1024 * 1024
@@ -599,7 +721,7 @@
         output_weight,
         stored_keys,
         stored_values,
-        seen,
+        lengths,
         adapter_down,
         down_first_moment,
         down_second_moment,
@@ -609,6 +731,14 @@
         up_second_moment,
         up_gradients[0],
     )
+    results = pl.pallas_call(
+        functools.partial(write_kernel, 7),
+        out_shape=[place(r.shape, r.dtype) for r in results],
+        in_specs=[whole] * 7,
+        out_specs=[whole] * 7,
+        scratch_shapes=[vm(r.shape, r.dtype) for r in results] + [dma((2, 7))],
+        compiler_params=pltpu.CompilerParams(vmem_limit_bytes=32 * 1024 * 1024),
+    )(*results)
     return (*results[:6], results[6].reshape(steps, rows, width))
 
 

time: 93.3 us -> 75.8 us (0.81)
  Pallas kernels: 79.1 us -> 68.1 us
  local copies, waits for them, and re-layouts: 13.2 us -> 6.67 us
    pallas_call x1, Pallas kernels: 79.1 us -> 66.1 us  [fused_shards(): pl.pallas_call(functools.partial(fused_kernel, z), out_shape=[place(down,...]
    unnamed x7 -> x14, local copies, waits for them, and re-layouts: 11.8 us -> 6.67 us
    pallas_call x0 -> x1, Pallas kernels: none -> 1.94 us  [fused_shards(): pl.pallas_call(functools.partial(write_kernel, 7), out_shape=[place(r.sha...]
    broadcast_in_dim x1 -> x0, local copies, waits for them, and re-layouts: 1.44 us -> none  [fused_shards(): jnp.broadcast_to(lengths[:, None, None], (rows, steps * group, z * context))]
where the time goes in v2:
time: 75.8 us; the launch traced here: 75.4 us
  Pallas kernels  68.1 us (90%)
  local copies, waits for them, and re-layouts  6.67 us (9%)
    pallas_call x1, Pallas kernels, fused_shards(): pl.pallas_call(functools.partial(fused_kernel, z), out_shape=[place(down,...  66.1 us
    unnamed x14, local copies, waits for them, and re-layouts  6.67 us
    pallas_call x1, Pallas kernels, fused_shards(): pl.pallas_call(functools.partial(write_kernel, 7), out_shape=[place(r.sha...  1.94 us

profile of v2, /device:TPU:0, one launch (start us, length us, event | category | flops | bytes accessed | tf_op | source)
XLA Modules:
  0.0 75.4 jit_solution(7666985285469243309)
XLA Ops:
  0.6 66.1 %shard_map.198 = (f32[64,1280]{1,0:T(8,128)}, f32[64,1280]{1,0:T(8,128)}, f32[64,1280]{1,0:T(8,128)}, f32[64,1024]{1,0:T(8,128)}, f32[64,1024]{1,0:T(8,128)}, /*...) custom-call(bf16[64,1280]{1,0:T(8,128)(2,1)} %bitcast.6, bf16[5120,1024]{1,0:T(8,128)(2,1)} %base_in.1, ...), custom_call_target="tpu_custom_call" | custom-call | tf_op jit(solution)/shard_map/pallas_call | solution.py:664
  66.8 0.0 copy-start
  66.8 1.0 %copy-done = f32[64,1280]{1,0:T(8,128)S(1)} copy-done((f32[64,1280]{1,0:T(8,128)S(1)}, f32[64,1280]{1,0:T(8,128)}, u32[]{:S(2)}) %copy-start) | copy-done | bytes 327704
  67.8 0.0 copy-start.1
  67.8 1.0 %copy-done.1 = f32[64,1280]{1,0:T(8,128)S(1)} copy-done((f32[64,1280]{1,0:T(8,128)S(1)}, f32[64,1280]{1,0:T(8,128)}, u32[]{:S(2)}) %copy-start.1) | copy-done | bytes 327704
  68.7 0.0 copy-start.2
  68.7 1.0 %copy-done.2 = f32[64,1280]{1,0:T(8,128)S(1)} copy-done((f32[64,1280]{1,0:T(8,128)S(1)}, f32[64,1280]{1,0:T(8,128)}, u32[]{:S(2)}) %copy-start.2) | copy-done | bytes 327704
  69.7 0.0 copy-start.3
  69.7 0.9 %copy-done.3 = f32[64,1024]{1,0:T(8,128)S(1)} copy-done((f32[64,1024]{1,0:T(8,128)S(1)}, f32[64,1024]{1,0:T(8,128)}, u32[]{:S(2)}) %copy-start.3) | copy-done | bytes 262168
  70.7 0.0 copy-start.4
  70.7 0.9 %copy-done.4 = f32[64,1024]{1,0:T(8,128)S(1)} copy-done((f32[64,1024]{1,0:T(8,128)S(1)}, f32[64,1024]{1,0:T(8,128)}, u32[]{:S(2)}) %copy-start.4) | copy-done | bytes 262168
  71.6 0.0 copy-start.5
  71.6 0.9 %copy-done.5 = f32[64,1024]{1,0:T(8,128)S(1)} copy-done((f32[64,1024]{1,0:T(8,128)S(1)}, f32[64,1024]{1,0:T(8,128)}, u32[]{:S(2)}) %copy-start.5) | copy-done | bytes 262168
  72.6 0.0 copy-start.6
  72.6 0.9 %copy-done.6 = bf16[64,1280]{1,0:T(8,128)(2,1)S(1)} copy-done((bf16[64,1280]{1,0:T(8,128)(2,1)S(1)}, bf16[64,1280]{1,0:T(8,128)(2,1)}, u32[]{:S(2)}) %copy-start.6) | copy-done | bytes 163864
  73.5 1.9 %shard_map.199 = (f32[64,1280]{1,0:T(8,128)}, f32[64,1280]{1,0:T(8,128)}, f32[64,1280]{1,0:T(8,128)}, f32[64,1024]{1,0:T(8,128)}, f32[64,1024]{1,0:T(8,128)}, /*...) custom-call(f32[64,1280]{1,0:T(8,128)S(1)} %copy-done, f32[64,1280]{1,0:T(8,128)S(1)} %copy-done.1, f32[64,1280]{1,0:T(8,128)S(1)} %copy-done.2, ...), custom_call_target="tpu_custom_call" | custom-call | tf_op jit(solution)/shard_map/pallas_call | solution.py:734
Async XLA Ops:
  66.8 1.0 %copy-start = (f32[64,1280]{1,0:T(8,128)S(1)}, f32[64,1280]{1,0:T(8,128)}, u32[]{:S(2)}) copy-start(f32[64,1280]{1,0:T(8,128)} %get-tuple-element.21.refs_0_) | copy-start | bytes 983044
  67.8 1.0 %copy-start.1 = (f32[64,1280]{1,0:T(8,128)S(1)}, f32[64,1280]{1,0:T(8,128)}, u32[]{:S(2)}) copy-start(f32[64,1280]{1,0:T(8,128)} %get-tuple-element.22.refs_1_) | copy-start | bytes 983044
  68.7 1.0 %copy-start.2 = (f32[64,1280]{1,0:T(8,128)S(1)}, f32[64,1280]{1,0:T(8,128)}, u32[]{:S(2)}) copy-start(f32[64,1280]{1,0:T(8,128)} %get-tuple-element.23.refs_2_) | copy-start | bytes 983044
  69.7 0.9 %copy-start.3 = (f32[64,1024]{1,0:T(8,128)S(1)}, f32[64,1024]{1,0:T(8,128)}, u32[]{:S(2)}) copy-start(f32[64,1024]{1,0:T(8,128)} %get-tuple-element.24.refs_3_) | copy-start | bytes 786436
  70.7 0.9 %copy-start.4 = (f32[64,1024]{1,0:T(8,128)S(1)}, f32[64,1024]{1,0:T(8,128)}, u32[]{:S(2)}) copy-start(f32[64,1024]{1,0:T(8,128)} %get-tuple-element.25.refs_4_) | copy-start | bytes 786436
  71.6 0.9 %copy-start.5 = (f32[64,1024]{1,0:T(8,128)S(1)}, f32[64,1024]{1,0:T(8,128)}, u32[]{:S(2)}) copy-start(f32[64,1024]{1,0:T(8,128)} %get-tuple-element.26.refs_5_) | copy-start | bytes 786436
  72.6 0.9 %copy-start.6 = (bf16[64,1280]{1,0:T(8,128)(2,1)S(1)}, bf16[64,1280]{1,0:T(8,128)(2,1)}, u32[]{:S(2)}) copy-start(bf16[64,1280]{1,0:T(8,128)(2,1)} %get-tuple-element.27.refs_6_) | copy-start | bytes 491524

commit v3 on v2

--- a/solution.py
+++ b/solution.py
@@ -212,6 +212,10 @@
     vu,
     gd,
     gu,
+    b1d,
+    b1u,
+    b2d,
+    b2u,
     g1d,
     g1u,
     g2d,
@@ -355,31 +359,45 @@
     load_ow = load(13, ow_in, ow_v)
     pl.semaphore_wait(barrier, shards_z + 1)
 
-    g1 = [
-        to_dp(0, mate, gd_in.at[theirs], g1d),
-        to_dp(1, mate, gu_in.at[theirs], g1u),
-    ]
     hop_start(1)
 
     load_gd.wait()
     load_gu.wait()
+    b1d[...] = gd[theirs, :].astype(BF16)
+    b1u[...] = gu[theirs, :].astype(BF16)
+    g1 = [to_dp(0, mate, b1d, g1d), to_dp(1, mate, b1u, g1u)]
     for copy in g1:
         copy.wait_recv()
-    g2d[...] = gd[mine, :] + g1d[...]
-    g2u[...] = gu[mine, :] + g1u[...]
+    g2d[...] = gd[mine, :] + g1d[...].astype(F32)
+    g2u[...] = gu[mine, :] + g1u[...].astype(F32)
+    b2d[...] = g2d[...].astype(BF16)
+    b2u[...] = g2u[...].astype(BF16)
     kept = quarter_rows(side)
     given = quarter_rows(1 - side)
-    g2 = [to_dp(2, across, g2d.at[given], r2d), to_dp(3, across, g2u.at[given], r2u)]
+    g2 = [to_dp(2, across, b2d.at[given], r2d), to_dp(3, across, b2u.at[given], r2u)]
     hop_arrive(1)
     hop_start(2)
+    parts_of_rows = 2
+    rows_each = q_rows.shape[0]
+    rows_part = rows_each // parts_of_rows
+
+    def send_caches(part):
+        cut = pl.ds(part * rows_part, rows_part)
+        return [
+            to_z(2 + 2 * part + i, d, source.at[peers[d], cut], held.at[t, cut])
+            for d in order
+            for i, (source, held) in enumerate(((keys_in, keys_v), (values_in, values_v)))
+        ]
+
+    sent_caches = [send_caches(0)]
     for copy in adam_loads:
         copy.wait()
     for copy in g2:
         copy.wait_recv()
     own = quarter_rows(quarter)
     next_to = quarter_rows(beside)
-    gsd[own, :] = g2d[kept, :] + r2d[...]
-    gsu[own, :] = g2u[kept, :] + r2u[...]
+    gsd[own, :] = (g2d[kept, :] + r2d[...].astype(F32)).astype(BF16)
+    gsu[own, :] = (g2u[kept, :] + r2u[...].astype(F32)).astype(BF16)
     gs = [
         to_dp(4, across, gsd.at[own], gsd.at[own]),
         to_dp(5, across, gsu.at[own], gsu.at[own]),
@@ -391,7 +409,7 @@
 
     def step_down(q):
         rows = quarter_rows(q)
-        new = moment_optimizer_update(pd[rows, :], md[rows, :], vd[rows, :], gsd[rows, :])
+        new = moment_optimizer_update(pd[rows, :], md[rows, :], vd[rows, :], gsd[rows, :].astype(F32))
         pd[rows, :], md[rows, :], vd[rows, :] = new
         high, low = split_high_low(new[0])
         factors[t, q, 0:qr, :] = high
@@ -401,19 +419,6 @@
     sent_factors = [to_z(0, d, factors.at[t, quarter], factors.at[t, quarter]) for d in order]
     hop_arrive(2)
     hop_start(3)
-    parts_of_rows = 2
-    rows_each = q_rows.shape[0]
-    rows_part = rows_each // parts_of_rows
-
-    def send_caches(part):
-        cut = pl.ds(part * rows_part, rows_part)
-        return [
-            to_z(2 + 2 * part + i, d, source.at[peers[d], cut], held.at[t, cut])
-            for d in order
-            for i, (source, held) in enumerate(((keys_in, keys_v), (values_in, values_v)))
-        ]
-
-    sent_caches = [send_caches(0)]
     for copy in gs:
         copy.wait_recv()
     gm += [
@@ -425,7 +430,7 @@
         copy.wait_recv()
     step_down(other * 2)
     step_down(other * 2 + 1)
-    new_up = moment_optimizer_update(pu[...], mu[...], vu[...], gsu[...])
+    new_up = moment_optimizer_update(pu[...], mu[...], vu[...], gsu[...].astype(F32))
     pu[...], mu[...], vu[...] = new_up
     stores = []
     for i, (a, b) in enumerate(
@@ -484,7 +489,6 @@
 
         lax.fori_loop(0, width // tile, body, 0)
 
-    query_block(t)
     passed = []
     crossed = []
     for d in order:
@@ -492,6 +496,7 @@
         slot = factors.at[sources[d], quarter]
         crossed.append(to_dp(10 + 3 * d, across, slot, slot))
         passed.append(to_dp(11 + 3 * d, mate, slot, slot))
+    query_block(t)
     for d in order:
         crossed[d].wait_recv()
         slot = factors.at[sources[d], beside]
@@ -682,14 +687,18 @@
             vm(up, F32),
             vm(down, F32),
             vm(up, F32),
+            vm(down_half, BF16),
+            vm(up_half, BF16),
+            vm(down_half, BF16),
+            vm(up_half, BF16),
+            vm(down_half, BF16),
+            vm(up_half, BF16),
             vm(down_half, F32),
             vm(up_half, F32),
-            vm(down_half, F32),
-            vm(up_half, F32),
-            vm((rank // 4, down[1]), F32),
-            vm((rank // 4, up[1]), F32),
-            vm(down, F32),
-            vm(up, F32),
+            vm((rank // 4, down[1]), BF16),
+            vm((rank // 4, up[1]), BF16),
+            vm(down, BF16),
+            vm(up, BF16),
             vm((z, 4, rank // 2, width), BF16),
             vm((4 * rank, columns), BF16),
             vm((z, flat, 2 * HEAD_SIZE), F32),
@@ -737,7 +746,7 @@
         in_specs=[whole] * 7,
         out_specs=[whole] * 7,
         scratch_shapes=[vm(r.shape, r.dtype) for r in results] + [dma((2, 7))],
-        compiler_params=pltpu.CompilerParams(vmem_limit_bytes=32 * 1024 * 1024),
+        compiler_params=pltpu.CompilerParams(vmem_limit_bytes=56 * 1024 * 1024),
     )(*results)
     return (*results[:6], results[6].reshape(steps, rows, width))
 

time: 75.8 us -> 68.8 us (0.908)
  local copies, waits for them, and re-layouts: 6.67 us -> 0 us
    unnamed x14 -> x0, local copies, waits for them, and re-layouts: 6.67 us -> none
where the time goes in v3:
time: 68.8 us; the launch traced here: 68.5 us
  Pallas kernels  67.8 us (99%)
    pallas_call x1, Pallas kernels, fused_shards(): pl.pallas_call(functools.partial(fused_kernel, z), out_shape=[place(down,...  65.5 us
    pallas_call x1, Pallas kernels, fused_shards(): pl.pallas_call(functools.partial(write_kernel, 7), out_shape=[place(r.sha...  2.35 us

profile of v3, /device:TPU:0, one launch (start us, length us, event | category | flops | bytes accessed | tf_op | source)
XLA Modules:
  0.0 68.5 jit_solution(9508766055118745793)
XLA Ops:
  0.6 65.5 %shard_map.198 = (f32[64,1280]{1,0:T(8,128)}, f32[64,1280]{1,0:T(8,128)}, f32[64,1280]{1,0:T(8,128)}, f32[64,1024]{1,0:T(8,128)}, f32[64,1024]{1,0:T(8,128)}, /*...) custom-call(bf16[64,1280]{1,0:T(8,128)(2,1)} %bitcast.6, bf16[5120,1024]{1,0:T(8,128)(2,1)} %base_in.1, ...), custom_call_target="tpu_custom_call" | custom-call | tf_op jit(solution)/shard_map/pallas_call | solution.py:669
  66.1 2.3 %shard_map.199 = (f32[64,1280]{1,0:T(8,128)}, f32[64,1280]{1,0:T(8,128)}, f32[64,1280]{1,0:T(8,128)}, f32[64,1024]{1,0:T(8,128)}, f32[64,1024]{1,0:T(8,128)}, /*...) custom-call(f32[64,1280]{1,0:T(8,128)} %get-tuple-element.21.refs_0_, f32[64,1280]{1,0:T(8,128)} %get-tuple-element.22.refs_1_, ...), custom_call_target="tpu_custom_call" | custom-call | tf_op jit(solution)/shard_map/pallas_call | solution.py:743

commit v4 on v2

--- a/solution.py
+++ b/solution.py
@@ -372,6 +372,19 @@
     g2 = [to_dp(2, across, g2d.at[given], r2d), to_dp(3, across, g2u.at[given], r2u)]
     hop_arrive(1)
     hop_start(2)
+    parts_of_rows = 2
+    rows_each = q_rows.shape[0]
+    rows_part = rows_each // parts_of_rows
+
+    def send_caches(part):
+        cut = pl.ds(part * rows_part, rows_part)
+        return [
+            to_z(2 + 2 * part + i, d, source.at[peers[d], cut], held.at[t, cut])
+            for d in order
+            for i, (source, held) in enumerate(((keys_in, keys_v), (values_in, values_v)))
+        ]
+
+    sent_caches = [send_caches(0)]
     for copy in adam_loads:
         copy.wait()
     for copy in g2:
@@ -401,19 +414,6 @@
     sent_factors = [to_z(0, d, factors.at[t, quarter], factors.at[t, quarter]) for d in order]
     hop_arrive(2)
     hop_start(3)
-    parts_of_rows = 2
-    rows_each = q_rows.shape[0]
-    rows_part = rows_each // parts_of_rows
-
-    def send_caches(part):
-        cut = pl.ds(part * rows_part, rows_part)
-        return [
-            to_z(2 + 2 * part + i, d, source.at[peers[d], cut], held.at[t, cut])
-            for d in order
-            for i, (source, held) in enumerate(((keys_in, keys_v), (values_in, values_v)))
-        ]
-
-    sent_caches = [send_caches(0)]
     for copy in gs:
         copy.wait_recv()
     gm += [
@@ -461,7 +461,6 @@
                 local_rows, kvw_v[:, at : at + HEAD_SIZE], preferred_element_type=F32
             )
     sent_kv = [to_z(1, d, kv_send.at[peers[d]], kv_recv.at[t]) for d in order]
-    sent_caches.append(send_caches(1))
 
     load_base.wait()
     q_acc[...] = jnp.zeros_like(q_acc)
@@ -484,7 +483,6 @@
 
         lax.fori_loop(0, width // tile, body, 0)
 
-    query_block(t)
     passed = []
     crossed = []
     for d in order:
@@ -492,6 +490,8 @@
         slot = factors.at[sources[d], quarter]
         crossed.append(to_dp(10 + 3 * d, across, slot, slot))
         passed.append(to_dp(11 + 3 * d, mate, slot, slot))
+    sent_caches.append(send_caches(1))
+    query_block(t)
     for d in order:
         crossed[d].wait_recv()
         slot = factors.at[sources[d], beside]
@@ -737,7 +737,7 @@
         in_specs=[whole] * 7,
         out_specs=[whole] * 7,
         scratch_shapes=[vm(r.shape, r.dtype) for r in results] + [dma((2, 7))],
-        compiler_params=pltpu.CompilerParams(vmem_limit_bytes=32 * 1024 * 1024),
+        compiler_params=pltpu.CompilerParams(vmem_limit_bytes=56 * 1024 * 1024),
     )(*results)
     return (*results[:6], results[6].reshape(steps, rows, width))
 

time: 75.8 us -> 68.2 us (0.90)
  local copies, waits for them, and re-layouts: 6.67 us -> 0 us
    unnamed x14 -> x0, local copies, waits for them, and re-layouts: 6.67 us -> none
    pallas_call x1, Pallas kernels: 66.1 us -> 65 us  [fused_shards(): pl.pallas_call(functools.partial(fused_kernel, z), out_shape=[place(down,...]
where the time goes in v4:
time: 68.2 us; the launch traced here: 68 us
  Pallas kernels  67.4 us (99%)
    pallas_call x1, Pallas kernels, fused_shards(): pl.pallas_call(functools.partial(fused_kernel, z), out_shape=[place(down,...  65 us
    pallas_call x1, Pallas kernels, fused_shards(): pl.pallas_call(functools.partial(write_kernel, 7), out_shape=[place(r.sha...  2.35 us

profile of v4, /device:TPU:0, one launch (start us, length us, event | category | flops | bytes accessed | tf_op | source)
XLA Modules:
  0.0 68.0 jit_solution(5579919154162057513)
XLA Ops:
  0.6 65.0 %shard_map.198 = (f32[64,1280]{1,0:T(8,128)}, f32[64,1280]{1,0:T(8,128)}, f32[64,1280]{1,0:T(8,128)}, f32[64,1024]{1,0:T(8,128)}, f32[64,1024]{1,0:T(8,128)}, /*...) custom-call(bf16[64,1280]{1,0:T(8,128)(2,1)} %bitcast.6, bf16[5120,1024]{1,0:T(8,128)(2,1)} %base_in.1, ...), custom_call_target="tpu_custom_call" | custom-call | tf_op jit(solution)/shard_map/pallas_call | solution.py:664
  65.7 2.3 %shard_map.199 = (f32[64,1280]{1,0:T(8,128)}, f32[64,1280]{1,0:T(8,128)}, f32[64,1280]{1,0:T(8,128)}, f32[64,1024]{1,0:T(8,128)}, f32[64,1024]{1,0:T(8,128)}, /*...) custom-call(f32[64,1280]{1,0:T(8,128)} %get-tuple-element.21.refs_0_, f32[64,1280]{1,0:T(8,128)} %get-tuple-element.22.refs_1_, ...), custom_call_target="tpu_custom_call" | custom-call | tf_op jit(solution)/shard_map/pallas_call | solution.py:734
